TPU v7x, 32 devices: a whole 2x2x4 slice. The times are simulated.
32 devices in a mesh: depth: 4 (over x, core), trans: 8 (over z, y).
Axes of the slice: x: 2, y: 2, z: 4, core: 2. Of those that a mesh axis runs over, the one named last changes fastest.
Arguments:
- screens: float32 [4, 2048, 2048], P('depth', 'trans'), may hold values from -1.5 to 1.5
- measured: bfloat16 [1, 2, 2048, 2048], P(None, None, 'trans'), may hold values from -4 to 4
- angle_index: int32 [1, 2], replicated, may hold values from -128 to 128
Outputs:
- screen_grad: float32 [4, 2048, 2048], P('depth', 'trans')
All inputs are finite; a program needn't handle non-finite values.
Results may differ from a plain program's by a relative error of at most 0.0003.
Values sent between devices are 32-bit elements; how exact they have to be, the bound alone decides.
A program may use at most 256 MiB of HBM per device.

v0:
```python
import functools
import math

import jax
import jax.numpy as jnp
from jax import lax
from jax.sharding import PartitionSpec as P

TWO_PI = 2.0 * math.pi


def from_behind(value, axis, steps):
    count = lax.axis_size(axis)
    first, last = (max(0, -steps), min(count, count - steps))
    return lax.ppermute(value, axis, [(source, source + steps) for source in range(first, last)])


def dft_table(length_all):
    positions = jnp.arange(length_all, dtype=jnp.int32)
    turn_count = positions[:, None] * positions[None, :] % length_all
    radians = -TWO_PI / length_all * turn_count.astype(jnp.float32)
    return (jnp.cos(radians), jnp.sin(radians))


def block_table(real_table, imag_table):
    upper = jnp.stack((real_table, imag_table), axis=1)
    lower = jnp.stack((-imag_table, real_table), axis=1)
    return jnp.stack((upper, lower), axis=0)


def line_factors(outer_grid, inner_grid, outer_size, length_all, orientation):
    twist = -TWO_PI / length_all * (inner_grid * outer_grid % length_all).astype(jnp.float32)
    frequency = outer_grid + outer_size * inner_grid
    signed_freq = jnp.where(frequency < length_all // 2, frequency, frequency - length_all)
    spread = (
        -orientation
        * TWO_PI
        / (8 * length_all)
        * (signed_freq * signed_freq % (8 * length_all)).astype(jnp.float32)
    )
    return (jnp.cos(twist), jnp.sin(twist), jnp.cos(spread), jnp.sin(spread))


def complex_product(left_spec, table_spec, out_spec, wave_field, table):
    form = "x" + left_spec + ",x" + table_spec[0] + "y" + table_spec[1] + "->y" + out_spec
    return jnp.einsum(
        form, wave_field, table, preferred_element_type=jnp.float32, precision=lax.Precision.HIGHEST
    )


def times_phase(complex_pair, cosine, sine_part):
    real_part = complex_pair[0] * cosine - complex_pair[1] * sine_part
    imag_part = complex_pair[0] * sine_part + complex_pair[1] * cosine
    return jnp.stack((real_part, imag_part))


def line_pass(wave_field, layout_spec, outer_size, inner_size, outer_grid, inner_grid, orientation):
    length_all = outer_size * inner_size
    outer_table = dft_table(outer_size)
    inner_table = dft_table(inner_size)
    outer_forward = block_table(outer_table[0], outer_table[1])
    inner_forward = block_table(inner_table[0], inner_table[1])
    inner_back = block_table(inner_table[0], -inner_table[1])
    outer_back = block_table(outer_table[0], -outer_table[1])
    twist_cos, twist_sin, spread_cos, spread_sin = line_factors(
        outer_grid, inner_grid, outer_size, length_all, orientation
    )
    spec_k = layout_spec.replace("p", "k")
    spec_m = spec_k.replace("q", "m")
    product = complex_product(layout_spec, "pk", spec_k, wave_field, outer_forward)
    wave_field = times_phase(product, twist_cos, twist_sin)
    product = complex_product(spec_k, "qm", spec_m, wave_field, inner_forward)
    wave_field = times_phase(product, spread_cos, spread_sin)
    product = complex_product(spec_m, "mq", spec_k, wave_field, inner_back)
    wave_field = times_phase(product, twist_cos, -twist_sin)
    product = complex_product(spec_k, "kp", layout_spec, wave_field, outer_back)
    return product / length_all


def x_pass(wave_field, orientation):
    old_shape = wave_field.shape
    grid_cells = old_shape[3]
    inner_size = min(128, grid_cells)
    outer_size = grid_cells // inner_size
    outer_grid = lax.broadcasted_iota(jnp.int32, (outer_size, inner_size), 0)
    inner_grid = lax.broadcasted_iota(jnp.int32, (outer_size, inner_size), 1)
    shaped = wave_field.reshape(old_shape[:3] + (outer_size, inner_size))
    result = line_pass(shaped, "brpq", outer_size, inner_size, outer_grid, inner_grid, orientation)
    return result.reshape(old_shape)


def y_pass(wave_field, orientation):
    inner_size = wave_field.shape[2]
    outer_size = wave_field.shape[3]
    outer_grid = lax.broadcasted_iota(jnp.int32, (inner_size, outer_size, 1), 1)
    inner_grid = lax.broadcasted_iota(jnp.int32, (inner_size, outer_size, 1), 0)
    return line_pass(
        wave_field, "bqpc", outer_size, inner_size, outer_grid, inner_grid, orientation
    )


def illumination(tilt_table, row_start, row_count, grid_cells):
    row_index = row_start + lax.broadcasted_iota(jnp.int32, (row_count, grid_cells), 0)
    column_index = lax.broadcasted_iota(jnp.int32, (row_count, grid_cells), 1)
    turn_count = (
        tilt_table[:, 0][:, None, None] * column_index + tilt_table[:, 1][:, None, None] * row_index
    ) % grid_cells
    radians = TWO_PI / grid_cells * turn_count.astype(jnp.float32)
    return jnp.stack((jnp.cos(radians), jnp.sin(radians)))


def rotate(wave_field, cosine, sine_part):
    real_part = wave_field[0] * cosine - wave_field[1] * sine_part
    imag_part = wave_field[0] * sine_part + wave_field[1] * cosine
    return jnp.stack((real_part, imag_part))


def rotate_back(wave_field, cosine, sine_part):
    real_part = wave_field[0] * cosine + wave_field[1] * sine_part
    imag_part = wave_field[1] * cosine - wave_field[0] * sine_part
    return jnp.stack((real_part, imag_part))


def grad_term(adjoint, kept_field):
    term = adjoint[1] * kept_field[0] - adjoint[0] * kept_field[1]
    return jnp.sum(term, axis=0)


def residual_of(exit_field, target):
    return exit_field - target.astype(jnp.float32)


def send_down(wave_field):
    return from_behind(wave_field, "depth", 1)


def send_up(wave_field):
    return from_behind(wave_field, "depth", -1)


def swap_narrow(wave_field, to_columns, trans_count):
    if to_columns:
        old_shape = wave_field.shape
        wave_field = wave_field.reshape(old_shape[:3] + (trans_count, old_shape[3] // trans_count))
    moved = lax.all_to_all(wave_field, "trans", split_axis=3, concat_axis=3, tiled=True)
    if to_columns:
        return moved
    old_shape = moved.shape
    return moved.reshape(old_shape[:3] + (old_shape[3] * old_shape[4],))


def apply_passes(wave_field, directions, orientation, swapper):
    for direction in directions:
        if direction == "x":
            wave_field = x_pass(wave_field, orientation)
        else:
            wave_field = swapper(wave_field, True)
            wave_field = y_pass(wave_field, orientation)
            wave_field = swapper(wave_field, False)
    return wave_field


def forward_section(wave_field, rotations, swapper):
    cosine, sine_part = rotations[0]
    wave_field = rotate(wave_field, cosine, sine_part)
    kept_fields = [wave_field]
    wave_field = apply_passes(wave_field, ("x", "y"), 1.0, swapper)
    return (wave_field, kept_fields)


def backward_section(adjoint, kept_fields, rotations, swapper):
    terms = [None] * len(rotations)
    for slice_at in reversed(range(len(rotations))):
        adjoint = apply_passes(adjoint, ("y", "x"), -1.0, swapper)
        terms[slice_at] = grad_term(adjoint, kept_fields[slice_at])
        cosine, sine_part = rotations[slice_at]
        adjoint = rotate_back(adjoint, cosine, sine_part)
    return (adjoint, terms)


def on_device(screens, measured, angle_index):
    slices, row_count, grid_cells = screens.shape
    angles = measured.shape[0]
    trans_count = lax.axis_size("trans")
    depth_count = lax.axis_size("depth")
    depth_at = lax.axis_index("depth")
    swapper = functools.partial(swap_narrow, trans_count=trans_count)
    row_start = lax.axis_index("trans") * row_count
    rotations = [(jnp.cos(screens[0]), jnp.sin(screens[0]))]
    segment_count = angles + depth_count - 1
    wave_field = jnp.zeros((2, 1, row_count, grid_cells), jnp.float32)
    history = []
    exit_fields = []
    for segment_at in range(segment_count):
        received = send_down(wave_field)
        incoming = illumination(angle_index, row_start, row_count, grid_cells)
        wave_field = jnp.where(depth_at == 0, incoming, received)
        wave_field, kept_fields = forward_section(wave_field, rotations, swapper)
        history.append(kept_fields[0])
        exit_fields.append(wave_field)
    stacked = jnp.stack(history)
    adjoint = jnp.zeros_like(wave_field)
    gradients = [jnp.zeros(stacked.shape[3:], jnp.float32)]
    for segment_at in range(segment_count):
        received = send_up(adjoint)
        exit_field = exit_fields[min(segment_at + depth_count - 1, segment_count - 1)]
        target = measured[min(segment_at, angles - 1)][:, None]
        seed_field = residual_of(exit_field, target)
        adjoint = jnp.where(depth_at == depth_count - 1, seed_field, received)
        source = jnp.clip(segment_at - depth_count + 1 + 2 * depth_at, 0, segment_count - 1)
        kept_fields = [lax.dynamic_index_in_dim(stacked, source, 0, keepdims=False)]
        adjoint, terms = backward_section(adjoint, kept_fields, rotations, swapper)
        angle_at = segment_at - (depth_count - 1 - depth_at)
        is_valid = (angle_at >= 0) & (angle_at < angles)
        gradients = [gradients[0] + jnp.where(is_valid, terms[0], 0.0)]
    return jnp.stack(gradients)


def solution(mesh):
    placed = (P("depth", "trans", None), P(None, None, "trans", None), P())
    return jax.shard_map(
        on_device, mesh=mesh, in_specs=placed, out_specs=P("depth", "trans", None), check_vma=False
    )
```

profile of v0, /device:TPU:1, one launch (start us, length us, event | category | flops | bytes accessed | tf_op | source)
XLA Modules:
  0.0 2318.0 jit_solution(18048977868230219431)
XLA Ops:
  11.7 9.0 fusion.333
  28.2 24.3 %collective-permute-done = f32[2,1,256,2048]{2,3,1,0:T(8,128)} collective-permute-done((f32[2,1,256,2048]{2,3,1,0:T(8,128)}, f32[2,1,256,2048]{2,3,1,0:T(8,128)}, u32[]{:S(2)}, u32[]{:S(2)}) %collective-permute-start) | collective-permute-done | bytes 4194336 | tf_op jit(solution)/shard_map/ppermute | solution.py:15
  121.3 62.0 %all-to-all-done = f32[2,1,256,8,256]{4,0,2,1,3:T(2,128)} async-done(((f32[2,1,256,8,256]{4,0,2,1,3:T(2,128)}), f32[2,1,256,8,256]{4,0,2,1,3:T(2,128)}, u32[]{:S(2)}, u32[]{:S(2)}) %all-to-all-start) | async-done | bytes 4194336 | tf_op jit(solution)/shard_map/all_to_all | solution.py:145
  183.3 7.9 fusion.177
  218.4 90.5 %all_to_all.80 = f32[2,1,256,8,256]{4,2,0,1,3:T(8,128)} all-to-all(f32[2,1,256,8,256]{4,2,0,1,3:T(8,128)S(1)} %copy.431), channel_id=1, replica_groups=mesh['depth'=4,'trans'=8] {'trans'}, dimensions={3} | all-to-all | bytes 8388608 | tf_op jit(solution)/shard_map/all_to_all | solution.py:145
  316.5 45.7 %collective-permute-done.1 = f32[2,1,256,2048]{2,3,0,1:T(8,128)S(1)} collective-permute-done((f32[2,1,256,2048]{2,3,0,1:T(8,128)}, f32[2,1,256,2048]{2,3,0,1:T(8,128)S(1)}, u32[]{:S(2)}, u32[]{:S(2)}) %collective-permute-start.1) | collective-permute-done | bytes 4194336 | tf_op jit(solution)/shard_map/ppermute | solution.py:15
  418.3 58.9 %all_to_all.81 = f32[2,1,256,8,256]{4,0,2,1,3:T(2,128)S(1)} all-to-all(f32[2,1,256,8,256]{4,0,2,1,3:T(2,128)S(1)} %copy.444), channel_id=1, replica_groups=mesh['depth'=4,'trans'=8] {'trans'}, dimensions={3} | all-to-all | bytes 8388608 | tf_op jit(solution)/shard_map/all_to_all | solution.py:145
  485.1 7.9 fusion.262
  509.5 83.0 %all_to_all.82 = f32[2,1,256,8,256]{4,2,0,1,3:T(8,128)} all-to-all(f32[2,1,256,8,256]{4,2,0,1,3:T(8,128)S(1)} %copy.450), channel_id=1, replica_groups=mesh['depth'=4,'trans'=8] {'trans'}, dimensions={3} | all-to-all | bytes 8388608 | tf_op jit(solution)/shard_map/all_to_all | solution.py:145
  599.9 45.7 %collective-permute-done.2 = f32[2,1,256,2048]{2,3,1,0:T(8,128)S(1)} collective-permute-done((f32[2,1,256,2048]{2,3,1,0:T(8,128)}, f32[2,1,256,2048]{2,3,1,0:T(8,128)S(1)}, u32[]{:S(2)}, u32[]{:S(2)}) %collective-permute-start.2) | collective-permute-done | bytes 4194336 | tf_op jit(solution)/shard_map/ppermute | solution.py:15
  700.1 59.0 %all_to_all.83 = f32[2,1,256,8,256]{4,0,2,1,3:T(2,128)S(1)} all-to-all(f32[2,1,256,8,256]{4,0,2,1,3:T(2,128)S(1)} %copy.461), channel_id=1, replica_groups=mesh['depth'=4,'trans'=8] {'trans'}, dimensions={3} | all-to-all | bytes 8388608 | tf_op jit(solution)/shard_map/all_to_all | solution.py:145
  791.7 83.0 %all_to_all.84 = f32[2,1,256,8,256]{4,2,0,1,3:T(8,128)} all-to-all(f32[2,1,256,8,256]{4,2,0,1,3:T(8,128)S(1)} %copy.467), channel_id=1, replica_groups=mesh['depth'=4,'trans'=8] {'trans'}, dimensions={3} | all-to-all | bytes 8388608 | tf_op jit(solution)/shard_map/all_to_all | solution.py:145
  882.2 45.7 %collective-permute-done.3 = f32[2,1,256,2048]{2,3,1,0:T(8,128)S(1)} collective-permute-done((f32[2,1,256,2048]{2,3,1,0:T(8,128)}, f32[2,1,256,2048]{2,3,1,0:T(8,128)S(1)}, u32[]{:S(2)}, u32[]{:S(2)}) %collective-permute-start.3) | collective-permute-done | bytes 4194336 | tf_op jit(solution)/shard_map/ppermute | solution.py:15
  982.5 59.0 %all_to_all.85 = f32[2,1,256,8,256]{4,0,2,1,3:T(2,128)S(1)} all-to-all(f32[2,1,256,8,256]{4,0,2,1,3:T(2,128)S(1)} %copy.478), channel_id=1, replica_groups=mesh['depth'=4,'trans'=8] {'trans'}, dimensions={3} | all-to-all | bytes 8388608 | tf_op jit(solution)/shard_map/all_to_all | solution.py:145
  1049.5 7.9 fusion.274
  1086.3 74.1 %all-to-all-done.7 = f32[2,1,256,8,256]{4,2,0,1,3:T(8,128)} async-done(((f32[2,1,256,8,256]{4,2,0,1,3:T(8,128)}), f32[2,1,256,8,256]{4,2,0,1,3:T(8,128)}, u32[]{:S(2)}, u32[]{:S(2)}) %all-to-all-start.7) | async-done | bytes 4194336 | tf_op jit(solution)/shard_map/all_to_all | solution.py:145
  1179.7 95.7 %all_to_all.86 = f32[2,1,256,8,256]{4,0,2,1,3:T(2,128)S(1)} all-to-all(f32[2,1,256,8,256]{4,0,2,1,3:T(2,128)} %copy.488), channel_id=1, replica_groups=mesh['depth'=4,'trans'=8] {'trans'}, dimensions={3} | all-to-all | bytes 8388608 | tf_op jit(solution)/shard_map/all_to_all | solution.py:145
  1283.3 7.9 fusion.280
  1308.0 96.4 %all_to_all.87 = f32[2,1,256,8,256]{4,2,0,1,3:T(8,128)S(1)} all-to-all(f32[2,1,256,8,256]{4,2,0,1,3:T(8,128)S(1)} %copy.494), channel_id=1, replica_groups=mesh['depth'=4,'trans'=8] {'trans'}, dimensions={3} | all-to-all | bytes 8388608 | tf_op jit(solution)/shard_map/all_to_all | solution.py:145
  1458.9 47.2 %collective-permute-done.5 = f32[2,1,256,2048]{2,3,1,0:T(8,128)S(1)} collective-permute-done((f32[2,1,256,2048]{2,3,1,0:T(8,128)S(1)}, f32[2,1,256,2048]{2,3,1,0:T(8,128)S(1)}, u32[]{:S(2)}, u32[]{:S(2)}) %collective-permute-start.5) | collective-permute-done | bytes 4194336 | tf_op jit(solution)/shard_map/ppermute | solution.py:15
  1516.0 57.9 %all_to_all.88 = f32[2,1,256,8,256]{4,0,2,1,3:T(2,128)S(1)} all-to-all(f32[2,1,256,8,256]{4,0,2,1,3:T(2,128)} %copy.510), channel_id=1, replica_groups=mesh['depth'=4,'trans'=8] {'trans'}, dimensions={3} | all-to-all | bytes 8388608 | tf_op jit(solution)/shard_map/all_to_all | solution.py:145
  1581.9 7.9 fusion.286
  1606.8 78.6 %all_to_all.89 = f32[2,1,256,8,256]{4,2,0,1,3:T(8,128)S(1)} all-to-all(f32[2,1,256,8,256]{4,2,0,1,3:T(8,128)S(1)} %copy.516), channel_id=1, replica_groups=mesh['depth'=4,'trans'=8] {'trans'}, dimensions={3} | all-to-all | bytes 8388608 | tf_op jit(solution)/shard_map/all_to_all | solution.py:145
  1739.0 56.6 %collective-permute-done.6 = f32[2,1,256,2048]{2,3,1,0:T(8,128)S(1)} collective-permute-done((f32[2,1,256,2048]{2,3,1,0:T(8,128)S(1)}, f32[2,1,256,2048]{2,3,1,0:T(8,128)S(1)}, u32[]{:S(2)}, u32[]{:S(2)}) %collective-permute-start.6) | collective-permute-done | bytes 4194336 | tf_op jit(solution)/shard_map/ppermute | solution.py:15
  1805.5 83.3 %all_to_all.90 = f32[2,1,256,8,256]{4,0,2,1,3:T(2,128)S(1)} all-to-all(f32[2,1,256,8,256]{4,0,2,1,3:T(2,128)} %copy.531), channel_id=1, replica_groups=mesh['depth'=4,'trans'=8] {'trans'}, dimensions={3} | all-to-all | bytes 8388608 | tf_op jit(solution)/shard_map/all_to_all | solution.py:145
  1921.4 52.0 %all_to_all.91 = f32[2,1,256,8,256]{4,2,0,1,3:T(8,128)S(1)} all-to-all(f32[2,1,256,8,256]{4,2,0,1,3:T(8,128)S(1)} %copy.537), channel_id=1, replica_groups=mesh['depth'=4,'trans'=8] {'trans'}, dimensions={3} | all-to-all | bytes 8388608 | tf_op jit(solution)/shard_map/all_to_all | solution.py:145
  2027.1 48.1 %collective-permute-done.7 = f32[2,1,256,2048]{2,3,1,0:T(8,128)S(1)} collective-permute-done((f32[2,1,256,2048]{2,3,1,0:T(8,128)S(1)}, f32[2,1,256,2048]{2,3,1,0:T(8,128)S(1)}, u32[]{:S(2)}, u32[]{:S(2)}) %collective-permute-start.7) | collective-permute-done | bytes 4194336 | tf_op jit(solution)/shard_map/ppermute | solution.py:15
  2085.0 57.0 %all_to_all.92 = f32[2,1,256,8,256]{4,0,2,1,3:T(2,128)S(1)} all-to-all(f32[2,1,256,8,256]{4,0,2,1,3:T(2,128)} %copy.552), channel_id=1, replica_groups=mesh['depth'=4,'trans'=8] {'trans'}, dimensions={3} | all-to-all | bytes 8388608 | tf_op jit(solution)/shard_map/all_to_all | solution.py:145
  2150.0 7.9 fusion.298
  2191.3 8.4 fusion.438
  2207.7 45.6 %all-to-all-done.15 = f32[2,1,256,8,256]{4,2,0,1,3:T(8,128)} async-done(((f32[2,1,256,8,256]{4,2,0,1,3:T(8,128)}), f32[2,1,256,8,256]{4,2,0,1,3:T(8,128)}, u32[]{:S(2)}, u32[]{:S(2)}) %all-to-all-start.15) | async-done | bytes 4194336 | tf_op jit(solution)/shard_map/all_to_all | solution.py:145
  2302.0 12.6 fusion.310
  (600 shorter events, 787.9 us)
Async XLA Ops:
  2.2 50.2 %collective-permute-start = (f32[2,1,256,2048]{2,3,1,0:T(8,128)}, f32[2,1,256,2048]{2,3,1,0:T(8,128)}, u32[]{:S(2)}, u32[]{:S(2)}) collective-permute-start(f32[2,1,256,2048]{2,3,1,0:T(8,128)} %broadcast.1766), channel_id=1, source_target_pairs={{0,8},{8,16},{16,24},{1,9},{9,17},{17,25},{2,10},{10,18},{18,26},{... | collective-permute-start | bytes 12582920 | tf_op jit(solution)/shard_map/ppermute | solution.py:15
  10.1 79.3 %copy-start.79 = (f32[16,128]{1,0:T(8,128)}, f32[16,128]{1,0:T(8,128)S(1)}, u32[]{:S(2)}) copy-start(f32[16,128]{1,0:T(8,128)S(1)} %fusion.429) | copy-start | bytes 24580
  10.2 59.1 %copy-start.87 = (f32[16,128]{1,0:T(8,128)}, f32[16,128]{1,0:T(8,128)S(1)}, u32[]{:S(2)}) copy-start(f32[16,128]{1,0:T(8,128)S(1)} %get-tuple-element.165) | copy-start | bytes 24580
  10.5 79.3 %copy-start.59 = (f32[1,16,2,16]{1,3,2,0:T(8,128)}, f32[1,16,2,16]{1,3,2,0:T(8,128)S(1)}, u32[]{:S(2)}) copy-start(f32[1,16,2,16]{1,3,2,0:T(8,128)S(1)} %get-tuple-element.139) | copy-start | bytes 6148
  10.5 79.3 %copy-start.67 = (f32[1,16,2,16]{1,3,2,0:T(8,128)}, f32[1,16,2,16]{1,3,2,0:T(8,128)S(1)}, u32[]{:S(2)}) copy-start(f32[1,16,2,16]{1,3,2,0:T(8,128)S(1)} %get-tuple-element.148) | copy-start | bytes 6148
  10.9 59.2 %copy-start.41 = (f32[1,128,2,128]{1,3,0,2:T(8,128)}, f32[1,128,2,128]{1,3,0,2:T(8,128)S(1)}, u32[]{:S(2)}) copy-start(f32[1,128,2,128]{1,3,0,2:T(8,128)S(1)} %get-tuple-element.134) | copy-start | bytes 393220
  10.9 59.2 %copy-start.49 = (f32[1,128,2,128]{1,3,0,2:T(8,128)}, f32[1,128,2,128]{1,3,0,2:T(8,128)S(1)}, u32[]{:S(2)}) copy-start(f32[1,128,2,128]{1,3,0,2:T(8,128)S(1)} %get-tuple-element.137) | copy-start | bytes 393220
  10.9 72.6 %copy-start.39 = (f32[1,128,2,128]{1,3,2,0:T(8,128)}, f32[1,128,2,128]{1,3,2,0:T(8,128)S(1)}, u32[]{:S(2)}) copy-start(f32[1,128,2,128]{1,3,2,0:T(8,128)S(1)} %get-tuple-element.138) | copy-start | bytes 393220
  11.6 63.4 %copy-start.149 = (f32[16,128]{1,0:T(8,128)}, f32[16,128]{1,0:T(8,128)S(1)}, u32[]{:S(2)}) copy-start(f32[16,128]{1,0:T(8,128)S(1)} %get-tuple-element.159) | copy-start | bytes 24580
  11.6 63.4 %copy-start.153 = (f32[16,128]{1,0:T(8,128)}, f32[16,128]{1,0:T(8,128)S(1)}, u32[]{:S(2)}) copy-start(f32[16,128]{1,0:T(8,128)S(1)} %get-tuple-element.160) | copy-start | bytes 24580
  107.8 75.6 %all-to-all-start = ((f32[2,1,256,8,256]{4,0,2,1,3:T(2,128)}), f32[2,1,256,8,256]{4,0,2,1,3:T(2,128)}, u32[]{:S(2)}, u32[]{:S(2)}) async-start(f32[2,1,256,8,256]{4,0,2,1,3:T(2,128)} %copy.423), calls=%async_computation | async-start | bytes 8388608 | tf_op jit(solution)/shard_map/all_to_all | solution.py:145
  314.3 47.9 %collective-permute-start.1 = (f32[2,1,256,2048]{2,3,0,1:T(8,128)}, f32[2,1,256,2048]{2,3,0,1:T(8,128)S(1)}, u32[]{:S(2)}, u32[]{:S(2)}) collective-permute-start(f32[2,1,256,2048]{2,3,0,1:T(8,128)} %bitcast.1346), channel_id=1, source_target_pairs={{0,8},{8,16},{16,24},{1,9},{9,17},{17,25},{2,10},{10,18},{18,26},{... | collective-permute-start | bytes 12582920 | tf_op jit(solution)/shard_map/ppermute | solution.py:15
  418.3 58.9 %copy-start.119 = (f32[1,8,2,8]{1,3,0,2:T(8,128)S(1)}, f32[1,8,2,8]{1,3,0,2:T(8,128)}, u32[]{:S(2)}) copy-start(f32[1,8,2,8]{1,3,0,2:T(8,128)} %copy.411) | copy-start | bytes 1540
  418.3 58.9 %copy-start.126 = (f32[1,8,2,8]{1,3,0,2:T(8,128)S(1)}, f32[1,8,2,8]{1,3,0,2:T(8,128)}, u32[]{:S(2)}) copy-start(f32[1,8,2,8]{1,3,0,2:T(8,128)} %copy.412) | copy-start | bytes 1540
  597.9 47.8 %collective-permute-start.2 = (f32[2,1,256,2048]{2,3,1,0:T(8,128)}, f32[2,1,256,2048]{2,3,1,0:T(8,128)S(1)}, u32[]{:S(2)}, u32[]{:S(2)}) collective-permute-start(f32[2,1,256,2048]{2,3,1,0:T(8,128)} %bitcast.1347), channel_id=1, source_target_pairs={{0,8},{8,16},{16,24},{1,9},{9,17},{17,25},{2,10},{10,18},{18,26},{... | collective-permute-start | bytes 12582920 | tf_op jit(solution)/shard_map/ppermute | solution.py:15
  700.1 59.1 %copy-start.120 = (f32[1,8,2,8]{1,3,0,2:T(8,128)S(1)}, f32[1,8,2,8]{1,3,0,2:T(8,128)}, u32[]{:S(2)}) copy-start(f32[1,8,2,8]{1,3,0,2:T(8,128)} %copy.411) | copy-start | bytes 1540
  700.1 59.1 %copy-start.127 = (f32[1,8,2,8]{1,3,0,2:T(8,128)S(1)}, f32[1,8,2,8]{1,3,0,2:T(8,128)}, u32[]{:S(2)}) copy-start(f32[1,8,2,8]{1,3,0,2:T(8,128)} %copy.412) | copy-start | bytes 1540
  880.1 47.8 %collective-permute-start.3 = (f32[2,1,256,2048]{2,3,1,0:T(8,128)}, f32[2,1,256,2048]{2,3,1,0:T(8,128)S(1)}, u32[]{:S(2)}, u32[]{:S(2)}) collective-permute-start(f32[2,1,256,2048]{2,3,1,0:T(8,128)} %bitcast.1348), channel_id=1, source_target_pairs={{0,8},{8,16},{16,24},{1,9},{9,17},{17,25},{2,10},{10,18},{18,26},{... | collective-permute-start | bytes 12582920 | tf_op jit(solution)/shard_map/ppermute | solution.py:15
  982.5 59.1 %copy-start.121 = (f32[1,8,2,8]{1,3,0,2:T(8,128)S(1)}, f32[1,8,2,8]{1,3,0,2:T(8,128)}, u32[]{:S(2)}) copy-start(f32[1,8,2,8]{1,3,0,2:T(8,128)} %copy.411) | copy-start | bytes 1540
  982.5 59.1 %copy-start.128 = (f32[1,8,2,8]{1,3,0,2:T(8,128)S(1)}, f32[1,8,2,8]{1,3,0,2:T(8,128)}, u32[]{:S(2)}) copy-start(f32[1,8,2,8]{1,3,0,2:T(8,128)} %copy.412) | copy-start | bytes 1540
  1075.9 84.5 %all-to-all-start.7 = ((f32[2,1,256,8,256]{4,2,0,1,3:T(8,128)}), f32[2,1,256,8,256]{4,2,0,1,3:T(8,128)}, u32[]{:S(2)}, u32[]{:S(2)}) async-start(f32[2,1,256,8,256]{4,2,0,1,3:T(8,128)} %copy.484), calls=%async_computation.7 | async-start | bytes 8388608 | tf_op jit(solution)/shard_map/all_to_all | solution.py:145
  1080.4 85.3 %collective-permute-start.4 = (f32[2,1,256,2048]{2,3,1,0:T(8,128)}, f32[2,1,256,2048]{2,3,1,0:T(8,128)}, u32[]{:S(2)}, u32[]{:S(2)}) collective-permute-start(f32[2,1,256,2048]{2,3,1,0:T(8,128)} %broadcast.1766), channel_id=1, source_target_pairs={{8,0},{16,8},{24,16},{9,1},{17,9},{25,17},{10,2},{18,10},{26,18},{... | collective-permute-start | bytes 12582920 | tf_op jit(solution)/shard_map/ppermute | solution.py:15
  1179.7 95.7 %copy-start.122 = (f32[1,8,2,8]{1,3,0,2:T(8,128)S(1)}, f32[1,8,2,8]{1,3,0,2:T(8,128)}, u32[]{:S(2)}) copy-start(f32[1,8,2,8]{1,3,0,2:T(8,128)} %copy.411) | copy-start | bytes 1540
  1179.7 95.7 %copy-start.129 = (f32[1,8,2,8]{1,3,0,2:T(8,128)S(1)}, f32[1,8,2,8]{1,3,0,2:T(8,128)}, u32[]{:S(2)}) copy-start(f32[1,8,2,8]{1,3,0,2:T(8,128)} %copy.412) | copy-start | bytes 1540
  1455.8 50.4 %collective-permute-start.5 = (f32[2,1,256,2048]{2,3,1,0:T(8,128)S(1)}, f32[2,1,256,2048]{2,3,1,0:T(8,128)S(1)}, u32[]{:S(2)}, u32[]{:S(2)}) collective-permute-start(f32[2,1,256,2048]{2,3,1,0:T(8,128)S(1)} %pad_maximum_fusion.2), channel_id=1, source_target_pairs={{8,0},{16,8},{24,16},{9,1},{17,9},{25,17},{10,2},{18,10},{26,18},{... | collective-permute-start | bytes 12582920 | tf_op jit(solution)/shard_map/ppermute | solution.py:15
  1736.4 59.2 %copy-start.5 = (f32[2,1,256,8,256]{2,4,3,0,1:T(8,128)S(1)}, f32[2,1,256,8,256]{2,4,3,0,1:T(8,128)}, u32[]{:S(2)}) copy-start(f32[2,1,256,8,256]{2,4,3,0,1:T(8,128)} %copy.485) | copy-start | bytes 12582916
  1736.4 59.2 %copy-start.12 = (bf16[1,2,256,2048]{2,3,1,0:T(8,128)(2,1)S(1)}, bf16[1,2,256,2048]{2,3,1,0:T(8,128)(2,1)}, u32[]{:S(2)}) copy-start(bf16[1,2,256,2048]{2,3,1,0:T(8,128)(2,1)} %copy.486) | copy-start | bytes 6291460
  1736.7 58.9 %collective-permute-start.6 = (f32[2,1,256,2048]{2,3,1,0:T(8,128)S(1)}, f32[2,1,256,2048]{2,3,1,0:T(8,128)S(1)}, u32[]{:S(2)}, u32[]{:S(2)}) collective-permute-start(f32[2,1,256,2048]{2,3,1,0:T(8,128)S(1)} %pad_maximum_fusion.3), channel_id=1, source_target_pairs={{8,0},{16,8},{24,16},{9,1},{17,9},{25,17},{10,2},{18,10},{26,18},{... | collective-permute-start | bytes 12582920 | tf_op jit(solution)/shard_map/ppermute | solution.py:15
  1805.5 83.3 %copy-start.124 = (f32[1,8,2,8]{1,3,0,2:T(8,128)S(1)}, f32[1,8,2,8]{1,3,0,2:T(8,128)}, u32[]{:S(2)}) copy-start(f32[1,8,2,8]{1,3,0,2:T(8,128)} %copy.411) | copy-start | bytes 1540
  1805.5 83.3 %copy-start.131 = (f32[1,8,2,8]{1,3,0,2:T(8,128)S(1)}, f32[1,8,2,8]{1,3,0,2:T(8,128)}, u32[]{:S(2)}) copy-start(f32[1,8,2,8]{1,3,0,2:T(8,128)} %copy.412) | copy-start | bytes 1540
  2024.7 50.4 %collective-permute-start.7 = (f32[2,1,256,2048]{2,3,1,0:T(8,128)S(1)}, f32[2,1,256,2048]{2,3,1,0:T(8,128)S(1)}, u32[]{:S(2)}, u32[]{:S(2)}) collective-permute-start(f32[2,1,256,2048]{2,3,1,0:T(8,128)S(1)} %pad_maximum_fusion.4), channel_id=1, source_target_pairs={{8,0},{16,8},{24,16},{9,1},{17,9},{25,17},{10,2},{18,10},{26,18},{... | collective-permute-start | bytes 12582920 | tf_op jit(solution)/shard_map/ppermute | solution.py:15
  2176.8 76.5 %all-to-all-start.15 = ((f32[2,1,256,8,256]{4,2,0,1,3:T(8,128)}), f32[2,1,256,8,256]{4,2,0,1,3:T(8,128)}, u32[]{:S(2)}, u32[]{:S(2)}) async-start(f32[2,1,256,8,256]{4,2,0,1,3:T(8,128)} %copy.558), calls=%async_computation.15 | async-start | bytes 8388608 | tf_op jit(solution)/shard_map/all_to_all | solution.py:145
  (145 other events, 1277.1 us)
where the time goes:
time: 2330 us; the launch traced here: 2320 us
  blocking collectives  954 us (41%)
  waiting for transfers between devices  495 us (21%)
  matrix products  378 us (16%)
  local copies, waits for them, and re-layouts  300 us (13%)
  other arithmetic  151 us (6%)
  starting transfers between devices  35.7 us (2%)
    all_to_all x13, blocking collectives, swap_narrow(): lax.all_to_all(wave_field, 'trans', split_axis=3, concat_axis=3, tiled=True)  954 us
    dot_general x64, matrix products, complex_product(): jnp.einsum(form, wave_field, table, preferred_element_type=jnp.float32, p...  378 us
    ppermute x8, waiting for transfers between devices, from_behind(): lax.ppermute(value, axis, [(source, source + steps) for source in range(f...  313 us
    all_to_all x3, waiting for transfers between devices, swap_narrow(): lax.all_to_all(wave_field, 'trans', split_axis=3, concat_axis=3, tiled=True)  182 us
    another operation x13, local copies, waits for them, and re-layouts  65 us
  transfers between devices with their start and end apart: 11, of which 10 were waited for; matrix products, arithmetic and copies ran while one was open for 2% of the time, Pallas kernels for 0%

commit v1 on v0

v1 whole, which is shorter than its diff:
```python
import functools
import math

import jax
import jax.numpy as jnp
import numpy as np
from jax import lax
from jax.experimental import pallas as pl
from jax.experimental.pallas import tpu as pltpu
from jax.sharding import PartitionSpec as P

TWO_PI = 2.0 * math.pi
LANES = 128
AXES = ("trans", "depth")


def as_pair(table):
    high = np.asarray(table, np.float32).astype(jnp.bfloat16)
    low = (np.asarray(table, np.float64) - high.astype(np.float64)).astype(jnp.bfloat16)
    return high, low


def tables_of(cells):
    outer = cells // LANES
    at = np.arange(LANES)
    radians = -TWO_PI / LANES * (at[:, None] * at[None, :] % LANES)
    c, s = np.cos(radians), np.sin(radians)
    ahead = np.block([[c, s], [-s, c]])
    back = np.block([[c, -s], [s, c]])
    k = np.arange(outer)[:, None]
    twist = -TWO_PI / cells * (k * at[None, :] % cells)
    freq = k + outer * at[None, :]
    signed = np.where(freq < cells // 2, freq, freq - cells)
    spread = -TWO_PI / (8 * cells) * (signed * signed % (8 * cells))
    phases = np.stack(
        [np.cos(twist), np.sin(twist), np.cos(spread) / cells, np.sin(spread) / cells]
    ).astype(np.float32)
    dft = np.stack([*as_pair(ahead), *as_pair(back)])
    return dft, phases


def small_dft(parts, sign):
    count = len(parts)
    if count == 1:
        return parts
    even = small_dft(parts[0::2], sign)
    odd = small_dft(parts[1::2], sign)
    low, high = [], []
    for k in range(count // 2):
        (er, ei), (r, i) = even[k], odd[k]
        turn = 8 * k / count
        if turn == 2:
            r, i = (-i, r) if sign > 0 else (i, -r)
        elif turn == 1:
            h = math.sqrt(0.5)
            r, i = (h * (r - sign * i), h * (i + sign * r))
        elif turn == 3:
            h = math.sqrt(0.5)
            r, i = (-h * (r + sign * i), h * (sign * r - i))
        elif k:
            c, s = math.cos(TWO_PI * k / count), sign * math.sin(TWO_PI * k / count)
            r, i = (r * c - i * s, r * s + i * c)
        low.append((er + r, ei + i))
        high.append((er - r, ei - i))
    return low + high


def product(value, dft_ref, high):
    top = value.astype(jnp.bfloat16)
    rest = (value - top.astype(jnp.float32)).astype(jnp.bfloat16)
    dot = functools.partial(jnp.dot, preferred_element_type=jnp.float32)
    return dot(top, dft_ref[high]) + (dot(top, dft_ref[high + 1]) + dot(rest, dft_ref[high]))


def chunk_pass(re, im, dft_ref, phase_ref, sign):
    lines, cells = re.shape
    outer = cells // LANES
    cut = [slice(LANES * a, LANES * (a + 1)) for a in range(outer)]
    parts = small_dft([(re[:, c], im[:, c]) for c in cut], -1)
    rows = []
    for k, (r, i) in enumerate(parts):
        c, s = phase_ref[0, k : k + 1], phase_ref[1, k : k + 1]
        rows.append(jnp.concatenate([r * c - i * s, r * s + i * c], 1))
    z = product(jnp.concatenate(rows, 0), dft_ref, 0)
    rows = []
    for k in range(outer):
        r, i = z[lines * k : lines * (k + 1), :LANES], z[lines * k : lines * (k + 1), LANES:]
        c, s = phase_ref[2, k : k + 1], sign * phase_ref[3, k : k + 1]
        rows.append(jnp.concatenate([r * c - i * s, r * s + i * c], 1))
    z = product(jnp.concatenate(rows, 0), dft_ref, 2)
    parts = []
    for k in range(outer):
        r, i = z[lines * k : lines * (k + 1), :LANES], z[lines * k : lines * (k + 1), LANES:]
        c, s = phase_ref[0, k : k + 1], phase_ref[1, k : k + 1]
        parts.append((r * c + i * s, i * c - r * s))
    parts = small_dft(parts, 1)
    return jnp.concatenate([p[0] for p in parts], 1), jnp.concatenate([p[1] for p in parts], 1)


def pass_kernel(sign, x_ref, dft_ref, phase_ref, out_ref):
    lines = x_ref.shape[1]
    step = min(16, lines)

    @pl.loop(0, lines // step)
    def _(at):
        here = pl.ds(pl.multiple_of(at * step, step), step)
        re, im = chunk_pass(x_ref[0, here], x_ref[1, here], dft_ref, phase_ref, sign)
        out_ref[0, here] = re
        out_ref[1, here] = im


def line_pass(field, tables, sign):
    whole = pl.BlockSpec(memory_space=pltpu.VMEM)
    return pl.pallas_call(
        functools.partial(pass_kernel, sign),
        out_shape=jax.ShapeDtypeStruct(field.shape, jnp.float32),
        in_specs=[whole] * 3,
        out_specs=whole,
        compiler_params=pltpu.CompilerParams(vmem_limit_bytes=32 << 20),
        name="line_pass",
    )(field, *tables)


def turn(field):
    two, lines, cells = field.shape
    count = cells // lines
    blocks = field.reshape(two * lines, cells).T.reshape(count, lines, two * lines)
    blocks = lax.all_to_all(blocks, AXES, split_axis=0, concat_axis=0, tiled=True)
    blocks = blocks.reshape(count, lines, two, lines)
    return blocks.transpose(2, 1, 0, 3).reshape(two, lines, cells)


def rotate(field, cosine, sine):
    return jnp.stack((field[0] * cosine - field[1] * sine, field[0] * sine + field[1] * cosine))


def illumination(angle_index, first, lines, cells):
    def wave(positions, tilt):
        turns = lax.rem(lax.rem(positions * tilt, cells) + cells, cells)
        radians = TWO_PI / cells * turns.astype(jnp.float32)
        return jnp.cos(radians), jnp.sin(radians)

    column = wave(jnp.arange(cells, dtype=jnp.int32), angle_index[0, 0])
    row = wave(first + jnp.arange(lines, dtype=jnp.int32), angle_index[0, 1])
    cc, cs = column[0][None], column[1][None]
    rc, rs = row[0][:, None], row[1][:, None]
    return jnp.stack((cc * rc - cs * rs, cc * rs + cs * rc))


def on_device(screens, measured, angle_index):
    depth_count = lax.axis_size("depth")
    held, cells = screens.shape[1:]
    lines = held // depth_count
    depth_at = lax.axis_index("depth")
    first = lax.axis_index("trans") * held + depth_at * lines
    tables = [jnp.asarray(t) for t in tables_of(cells)]

    spread_out = screens.reshape(depth_count, lines, cells)
    own = lax.all_to_all(spread_out, "depth", split_axis=0, concat_axis=0, tiled=True)
    odd = turn(own[1::2])
    phase = [odd[g // 2] if g % 2 else own[g] for g in range(depth_count)]
    cosine, sine = [jnp.cos(p) for p in phase], [jnp.sin(p) for p in phase]

    field = illumination(angle_index, first, lines, cells)
    kept = []
    for g in range(depth_count):
        field = rotate(field, cosine[g], sine[g])
        kept.append(field)
        field = line_pass(turn(line_pass(field, tables, 1.0)), tables, 1.0)
    target = lax.dynamic_slice_in_dim(measured[0], depth_at * lines, lines, 1)
    field = field - target.astype(jnp.float32)
    grads = [None] * depth_count
    for g in reversed(range(depth_count)):
        field = line_pass(turn(line_pass(field, tables, -1.0)), tables, -1.0)
        grads[g] = field[1] * kept[g][0] - field[0] * kept[g][1]
        field = rotate(field, cosine[g], -sine[g])
    odd = turn(jnp.stack(grads[1::2]))
    rows = jnp.stack([odd[g // 2] if g % 2 else grads[g] for g in range(depth_count)])
    out = lax.all_to_all(rows, "depth", split_axis=0, concat_axis=0, tiled=True)
    return out.reshape(1, held, cells)


def solution(mesh):
    placed = (P("depth", "trans", None), P(None, None, "trans", None), P())
    return jax.shard_map(
        on_device, mesh=mesh, in_specs=placed, out_specs=P("depth", "trans", None), check_vma=False
    )
```

time: 2330 us -> 497 us (0.21)
  blocking collectives: 954 us -> 148 us
  matrix products: 378 us -> 0 us
  waiting for transfers between devices: 495 us -> 146 us
  local copies, waits for them, and re-layouts: 300 us -> 102 us
  other arithmetic: 151 us -> 15.3 us
  Pallas kernels: 0 us -> 43.5 us
    all_to_all x13 -> x5, blocking collectives: 954 us -> 148 us  [the longest x4 120 us: turn(): lax.all_to_all(blocks, AXES, split_axis=0, concat_axis=0, tiled=True)]
    dot_general x64 -> x0, matrix products: 378 us -> none  [complex_product(): jnp.einsum(form, wave_field, table, preferred_element_type=jnp.float32, p...]
    ppermute x8 -> x0, waiting for transfers between devices: 313 us -> none  [from_behind(): lax.ppermute(value, axis, [(source, source + steps) for source in range(f...]
    another operation x33 -> x0, local copies, waits for them, and re-layouts: 137 us -> none
    another operation x60 -> x9, other arithmetic: 55.8 us -> 0.81 us  [the longest x7 0.54 us: rotate(): jnp.stack((field[0] * cosine - field[1] * sine, field[0] * sine + field[1...]
    pallas_call x0 -> x16, Pallas kernels: none -> 43.5 us  [line_pass(): pl.pallas_call(functools.partial(pass_kernel, sign), out_shape=jax.ShapeD...]
    all_to_all x8 -> x0, local copies, waits for them, and re-layouts: 41.2 us -> none  [swap_narrow(): lax.all_to_all(wave_field, 'trans', split_axis=3, concat_axis=3, tiled=True)]
    all_to_all x3 -> x7, waiting for transfers between devices: 182 us -> 146 us  [the longest x6 124 us: turn(): lax.all_to_all(blocks, AXES, split_axis=0, concat_axis=0, tiled=True)]
  transfers between devices with their start and end apart: 11 -> 7, of which waited for: 10 -> 7; matrix products, arithmetic and copies ran while one was open for 2% -> 5% of each run, Pallas kernels for 0% -> 1%
where the time goes in v1:
time: 497 us; the launch traced here: 492 us
  blocking collectives  148 us (30%)
  waiting for transfers between devices  146 us (29%)
  local copies, waits for them, and re-layouts  102 us (21%)
  Pallas kernels  43.5 us (9%)
  starting transfers between devices  35.3 us (7%)
  other arithmetic  15.3 us (3%)
    all_to_all x6, waiting for transfers between devices, turn(): lax.all_to_all(blocks, AXES, split_axis=0, concat_axis=0, tiled=True)  124 us
    all_to_all x4, blocking collectives, turn(): lax.all_to_all(blocks, AXES, split_axis=0, concat_axis=0, tiled=True)  120 us
    pallas_call x16, Pallas kernels, line_pass(): pl.pallas_call(functools.partial(pass_kernel, sign), out_shape=jax.ShapeD...  43.5 us
    all_to_all x6, starting transfers between devices, turn(): lax.all_to_all(blocks, AXES, split_axis=0, concat_axis=0, tiled=True)  30.9 us
    reshape x11, local copies, waits for them, and re-layouts, turn(): blocks = blocks.reshape(count, lines, two, lines)  28.6 us
    all_to_all x1, blocking collectives, on_device(): out = lax.all_to_all(rows, 'depth', split_axis=0, concat_axis=0, tiled=True)  28.4 us
    all_to_all x1, waiting for transfers between devices, on_device(): lax.all_to_all(spread_out, 'depth', split_axis=0, concat_axis=0, tiled=True)  22.6 us
    transpose x8, local copies, waits for them, and re-layouts, turn(): return blocks.transpose(2, 1, 0, 3).reshape(two, lines, cells)  20.6 us
  transfers between devices with their start and end apart: 7, of which 7 were waited for; matrix products, arithmetic and copies ran while one was open for 5% of the time, Pallas kernels for 1%

profile of v1, /device:TPU:1, one launch (start us, length us, event | category | flops | bytes accessed | tf_op | source)
XLA Modules:
  0.0 491.8 jit_solution(16530367340007417800)
XLA Ops:
  0.0 4.4 all-to-all-start
  6.3 22.6 %all-to-all-done = f32[4,64,2048]{2,1,0:T(8,128)S(1)} async-done(((f32[4,64,2048]{2,1,0:T(8,128)}), f32[4,64,2048]{2,1,0:T(8,128)S(1)}, u32[]{:S(2)}, u32[]{:S(2)}) %all-to-all-start) | async-done | bytes 2097184 | tf_op jit(solution)/shard_map/all_to_all | solution.py:159
  36.1 6.7 %all-to-all-start.1 = ((f32[32,64,128]{2,1,0:T(8,128)}), f32[32,64,128]{2,1,0:T(8,128)}, u32[]{:S(2)}, u32[]{:S(2)}) async-start(f32[32,64,128]{2,1,0:T(8,128)} %bitcast.107), calls=%async_computation.1 | async-start | bytes 2097152 | tf_op jit(solution)/shard_map/all_to_all | solution.py:128
  46.4 21.8 %all-to-all-done.1 = f32[32,64,128]{2,1,0:T(8,128)} async-done(((f32[32,64,128]{2,1,0:T(8,128)}), f32[32,64,128]{2,1,0:T(8,128)}, u32[]{:S(2)}, u32[]{:S(2)}) %all-to-all-start.1) | async-done | bytes 1048608 | tf_op jit(solution)/shard_map/all_to_all | solution.py:128
  68.2 5.1 %all-to-all-start.2 = ((f32[32,64,128]{2,1,0:T(8,128)}), f32[32,64,128]{2,1,0:T(8,128)}, u32[]{:S(2)}, u32[]{:S(2)}) async-start(f32[32,64,128]{2,1,0:T(8,128)} %bitcast.9), calls=%async_computation.2 | async-start | bytes 2097152 | tf_op jit(solution)/shard_map/all_to_all | solution.py:128
  80.4 2.7 line_pass.17
  83.2 15.3 %all-to-all-done.2 = f32[32,64,128]{2,1,0:T(8,128)} async-done(((f32[32,64,128]{2,1,0:T(8,128)}), f32[32,64,128]{2,1,0:T(8,128)}, u32[]{:S(2)}, u32[]{:S(2)}) %all-to-all-start.2) | async-done | bytes 1048608 | tf_op jit(solution)/shard_map/all_to_all | solution.py:128
  98.4 3.4 reshape.529
  101.8 2.8 copy.52
  104.6 8.2 %slice_sine_fusion.1 = (f32[1,64,32,64]{3,2,1,0:T(8,128)S(1)}, f32[1,64,32,64]{3,2,1,0:T(8,128)}, f32[1,64,32,64]{3,2,1,0:T(8,128)}, f32[1,64,32,64]{3,2,1,0:T(8,128)}) fusion(f32[2,64,32,64]{3,2,1,0:T(8,128)S(1)} %bitcast.95), kind=kLoop, calls=%fused_computation.13 | loop fusion | bytes 3145728 | tf_op jit(solution)/shard_map/sin | solution.py:162
  115.9 2.7 line_pass.18
  118.9 30.3 %all_to_all.60 = f32[32,64,128]{2,1,0:T(8,128)} all-to-all(f32[32,64,128]{2,1,0:T(8,128)S(1)} %bitcast.109), channel_id=1, replica_groups=mesh['depth'=4,'trans'=8] {'trans','depth'}, dimensions={0} | all-to-all | bytes 2097152 | tf_op jit(solution)/shard_map/all_to_all | solution.py:128
  156.4 2.7 line_pass.19
  159.1 3.3 multiply_subtract_fusion.7
  167.7 4.6 all-to-all-start.4
  174.6 23.1 %all-to-all-done.4 = f32[32,64,128]{2,1,0:T(8,128)} async-done(((f32[32,64,128]{2,1,0:T(8,128)}), f32[32,64,128]{2,1,0:T(8,128)}, u32[]{:S(2)}, u32[]{:S(2)}) %all-to-all-start.4) | async-done | bytes 1048608 | tf_op jit(solution)/shard_map/all_to_all | solution.py:128
  204.9 2.7 line_pass.21
  212.9 4.9 %all-to-all-start.5 = ((f32[32,64,128]{2,1,0:T(8,128)}), f32[32,64,128]{2,1,0:T(8,128)}, u32[]{:S(2)}, u32[]{:S(2)}) async-start(f32[32,64,128]{2,1,0:T(8,128)} %bitcast.21), calls=%async_computation.5 | async-start | bytes 2097152 | tf_op jit(solution)/shard_map/all_to_all | solution.py:128
  217.8 25.2 %all-to-all-done.5 = f32[32,64,128]{2,1,0:T(8,128)} async-done(((f32[32,64,128]{2,1,0:T(8,128)}), f32[32,64,128]{2,1,0:T(8,128)}, u32[]{:S(2)}, u32[]{:S(2)}) %all-to-all-start.5) | async-done | bytes 1048608 | tf_op jit(solution)/shard_map/all_to_all | solution.py:128
  250.2 2.7 line_pass.23
  257.1 29.8 %all_to_all.61 = f32[32,64,128]{2,1,0:T(8,128)} all-to-all(f32[32,64,128]{2,1,0:T(8,128)S(1)} %bitcast.110), channel_id=1, replica_groups=mesh['depth'=4,'trans'=8] {'trans','depth'}, dimensions={0} | all-to-all | bytes 2097152 | tf_op jit(solution)/shard_map/all_to_all | solution.py:128
  294.1 2.7 line_pass.25
  298.0 2.7 line_pass.26
  301.1 30.0 %all_to_all.62 = f32[32,64,128]{2,1,0:T(8,128)} all-to-all(f32[32,64,128]{2,1,0:T(8,128)S(1)} %bitcast.111), channel_id=1, replica_groups=mesh['depth'=4,'trans'=8] {'trans','depth'}, dimensions={0} | all-to-all | bytes 2097152 | tf_op jit(solution)/shard_map/all_to_all | solution.py:128
  341.0 4.1 multiply_subtract_fusion.4
  348.2 29.8 %all_to_all.63 = f32[32,64,128]{2,1,0:T(8,128)} all-to-all(f32[32,64,128]{2,1,0:T(8,128)S(1)} %bitcast.112), channel_id=1, replica_groups=mesh['depth'=4,'trans'=8] {'trans','depth'}, dimensions={0} | all-to-all | bytes 2097152 | tf_op jit(solution)/shard_map/all_to_all | solution.py:128
  390.5 4.5 all-to-all-start.10
  395.2 2.7 line_pass.30
  399.2 21.2 %all-to-all-done.10 = f32[32,64,128]{2,1,0:T(8,128)S(1)} async-done(((f32[32,64,128]{2,1,0:T(8,128)}), f32[32,64,128]{2,1,0:T(8,128)S(1)}, u32[]{:S(2)}, u32[]{:S(2)}) %all-to-all-start.10) | async-done | bytes 1048608 | tf_op jit(solution)/shard_map/all_to_all | solution.py:128
  421.4 5.0 %all-to-all-start.9 = ((f32[32,64,128]{2,1,0:T(8,128)}), f32[32,64,128]{2,1,0:T(8,128)}, u32[]{:S(2)}, u32[]{:S(2)}) async-start(f32[32,64,128]{2,1,0:T(8,128)} %bitcast.106), calls=%async_computation.9 | async-start | bytes 2097152 | tf_op jit(solution)/shard_map/all_to_all | solution.py:128
  434.5 17.1 %all-to-all-done.9 = f32[32,64,128]{2,1,0:T(8,128)} async-done(((f32[32,64,128]{2,1,0:T(8,128)}), f32[32,64,128]{2,1,0:T(8,128)}, u32[]{:S(2)}, u32[]{:S(2)}) %all-to-all-start.9) | async-done | bytes 1048608 | tf_op jit(solution)/shard_map/all_to_all | solution.py:128
  461.8 28.4 %all_to_all.64 = f32[4,64,2048]{2,1,0:T(8,128)S(1)} all-to-all(f32[4,64,2048]{2,1,0:T(8,128)S(1)} %pad_maximum_fusion), channel_id=1, replica_groups=mesh['depth'=4,'trans'=8] {'depth'}, dimensions={0} | all-to-all | bytes 4194304 | tf_op jit(solution)/shard_map/all_to_all | solution.py:179
  (145 shorter events, 117.5 us)
Async XLA Ops:
  0.0 4.4 copy-start.35
  0.0 28.9 %all-to-all-start = ((f32[4,64,2048]{2,1,0:T(8,128)}), f32[4,64,2048]{2,1,0:T(8,128)S(1)}, u32[]{:S(2)}, u32[]{:S(2)}) async-start(f32[4,64,2048]{2,1,0:T(8,128)} %bitcast.114), calls=%async_computation | async-start | bytes 4194304 | tf_op jit(solution)/shard_map/all_to_all | solution.py:159
  4.4 27.6 %copy-start = (bf16[4,256,256]{2,1,0:T(8,128)(2,1)S(1)}, bf16[4,256,256]{2,1,0:T(8,128)(2,1)}, u32[]{:S(2)}) copy-start(bf16[4,256,256]{2,1,0:T(8,128)(2,1)} %constant.34.clone.dft_ref) | copy-start | bytes 1572868
  4.4 27.6 %copy-start.1 = (f32[4,16,128]{2,1,0:T(8,128)S(1)}, f32[4,16,128]{2,1,0:T(8,128)}, u32[]{:S(2)}) copy-start(f32[4,16,128]{2,1,0:T(8,128)} %constant.35.clone.phase_ref) | copy-start | bytes 98308
  28.9 2.0 copy-start.2
  36.1 6.8 %copy-start.3 = (f32[4,64,2048]{2,1,0:T(8,128)S(1)}, f32[4,64,2048]{2,1,0:T(8,128)}, u32[]{:S(2)}) copy-start(f32[4,64,2048]{2,1,0:T(8,128)} %copy-done.2) | copy-start | bytes 6291460
  36.1 32.1 %all-to-all-start.1 = ((f32[32,64,128]{2,1,0:T(8,128)}), f32[32,64,128]{2,1,0:T(8,128)}, u32[]{:S(2)}, u32[]{:S(2)}) async-start(f32[32,64,128]{2,1,0:T(8,128)} %bitcast.107), calls=%async_computation.1 | async-start | bytes 2097152 | tf_op jit(solution)/shard_map/all_to_all | solution.py:128
  68.2 30.2 %all-to-all-start.2 = ((f32[32,64,128]{2,1,0:T(8,128)}), f32[32,64,128]{2,1,0:T(8,128)}, u32[]{:S(2)}, u32[]{:S(2)}) async-start(f32[32,64,128]{2,1,0:T(8,128)} %bitcast.9), calls=%async_computation.2 | async-start | bytes 2097152 | tf_op jit(solution)/shard_map/all_to_all | solution.py:128
  115.0 3.6 copy-start.14
  166.4 5.9 %copy-start.28 = (f32[1,64,32,64]{3,2,1,0:T(8,128)S(1)}, f32[1,64,32,64]{3,2,1,0:T(8,128)}, u32[]{:S(2)}) copy-start(f32[1,64,32,64]{3,2,1,0:T(8,128)} %get-tuple-element.22) | copy-start | bytes 1572868
  167.7 5.8 %copy-start.27 = (f32[1,64,32,64]{3,2,1,0:T(8,128)S(1)}, f32[1,64,32,64]{3,2,1,0:T(8,128)}, u32[]{:S(2)}) copy-start(f32[1,64,32,64]{3,2,1,0:T(8,128)} %get-tuple-element.23) | copy-start | bytes 1572868
  167.7 30.0 %all-to-all-start.4 = ((f32[32,64,128]{2,1,0:T(8,128)}), f32[32,64,128]{2,1,0:T(8,128)}, u32[]{:S(2)}, u32[]{:S(2)}) async-start(f32[32,64,128]{2,1,0:T(8,128)} %bitcast.17), calls=%async_computation.4 | async-start | bytes 2097152 | tf_op jit(solution)/shard_map/all_to_all | solution.py:128
  204.9 2.8 copy-start.6
  204.9 2.8 copy-start.8
  212.9 30.1 %all-to-all-start.5 = ((f32[32,64,128]{2,1,0:T(8,128)}), f32[32,64,128]{2,1,0:T(8,128)}, u32[]{:S(2)}, u32[]{:S(2)}) async-start(f32[32,64,128]{2,1,0:T(8,128)} %bitcast.21), calls=%async_computation.5 | async-start | bytes 2097152 | tf_op jit(solution)/shard_map/all_to_all | solution.py:128
  294.1 2.8 copy-start.7
  294.1 2.8 copy-start.9
  294.1 2.8 copy-start.19
  294.1 2.8 copy-start.21
  338.2 2.8 copy-start.23
  338.2 2.8 copy-start.25
  385.1 2.8 copy-start.5
  385.1 2.8 copy-start.15
  385.1 2.8 copy-start.17
  389.2 5.9 %copy-start.31 = (f32[1,64,2048]{2,1,0:T(8,128)S(1)}, f32[1,64,2048]{2,1,0:T(8,128)}, u32[]{:S(2)}) copy-start(f32[1,64,2048]{2,1,0:T(8,128)} %get-tuple-element.11) | copy-start | bytes 1572868
  390.5 4.5 copy-start.32
  390.5 29.9 %all-to-all-start.10 = ((f32[32,64,128]{2,1,0:T(8,128)}), f32[32,64,128]{2,1,0:T(8,128)S(1)}, u32[]{:S(2)}, u32[]{:S(2)}) async-start(f32[32,64,128]{2,1,0:T(8,128)} %bitcast.42), calls=%async_computation.10 | async-start | bytes 2097152 | tf_op jit(solution)/shard_map/all_to_all | solution.py:128
  421.4 30.2 %all-to-all-start.9 = ((f32[32,64,128]{2,1,0:T(8,128)}), f32[32,64,128]{2,1,0:T(8,128)}, u32[]{:S(2)}, u32[]{:S(2)}) async-start(f32[32,64,128]{2,1,0:T(8,128)} %bitcast.106), calls=%async_computation.9 | async-start | bytes 2097152 | tf_op jit(solution)/shard_map/all_to_all | solution.py:128
  458.7 2.8 copy-start.11
  458.7 2.8 copy-start.13
  458.7 2.9 copy-start.33
  458.7 2.9 copy-start.34
  (11 other events, 10.8 us)

commit v2 on v1

--- a/solution.py
+++ b/solution.py
@@ -11,7 +11,6 @@
 
 TWO_PI = 2.0 * math.pi
 LANES = 128
-AXES = ("trans", "depth")
 
 
 def as_pair(table):
@@ -97,41 +96,255 @@
     return jnp.concatenate([p[0] for p in parts], 1), jnp.concatenate([p[1] for p in parts], 1)
 
 
-def pass_kernel(sign, x_ref, dft_ref, phase_ref, out_ref):
-    lines = x_ref.shape[1]
+def cos_sin(x):
+    y = x * x
+    c = jnp.full_like(x, 1.0 / math.factorial(16))
+    for n in range(14, -1, -2):
+        c = c * -y + 1.0 / math.factorial(n)
+    s = jnp.full_like(x, 1.0 / math.factorial(15))
+    for n in range(13, 0, -2):
+        s = s * -y + 1.0 / math.factorial(n)
+    return c, s * x
+
+
+def mega_kernel(
+    depth_count,
+    screens_ref, wave_ref, target_ref, dft_ref, phase_ref,
+    out_ref,
+    field, result, kept, angle, grads, send, recv,
+    send_sem, recv_sem, out_sem, in_sem, back_out_sem, back_in_sem,
+):
+    _, lines, cells = wave_ref.shape
+    count = cells // lines
+    per_tile = max(1, LANES // lines)
+    depth_at, trans_at = lax.axis_index("depth"), lax.axis_index("trans")
+    me = trans_at * depth_count + depth_at
     step = min(16, lines)
 
-    @pl.loop(0, lines // step)
+    def device(at):
+        return {"trans": at // depth_count, "depth": at % depth_count}
+
+    def remote(slot, to, owner):
+        return pltpu.make_async_remote_copy(
+            src_ref=send.at[slot, to],
+            dst_ref=recv.at[slot, owner],
+            send_sem=send_sem.at[slot, to],
+            recv_sem=recv_sem.at[slot, owner],
+            device_id=device(to),
+            device_id_type=pl.DeviceIdType.MESH,
+        )
+
+    def turn_start(slot, top, bottom):
+        tiles = cells // LANES
+
+        @pl.loop(0, tiles)
+        def _(turn_at):
+            tile = lax.rem(me * lines // LANES + turn_at, tiles)
+            cols = pl.ds(pl.multiple_of(tile * LANES, LANES), LANES)
+            block = jnp.concatenate([top[:, cols], bottom[:, cols]], 0).T
+            for part in range(per_tile):
+                to = tile * per_tile + part
+                send[slot, to] = block[part * lines : (part + 1) * lines]
+
+                @pl.when(to != me)
+                def _():
+                    remote(slot, to, me).start()
+
+        recv[slot, me] = send[slot, me]
+
+    def turn_wait(slot):
+        @pl.loop(0, count)
+        def _(at):
+            @pl.when(at != me)
+            def _():
+                remote(slot, at, at).wait_recv()
+                remote(slot, at, at).wait_send()
+
+    def arrived(slot, here):
+        blocks = [recv[slot, at, here] for at in range(count)]
+        return (
+            jnp.concatenate([b[:, :lines] for b in blocks], 1),
+            jnp.concatenate([b[:, lines:] for b in blocks], 1),
+        )
+
+    def chunks(body):
+        @pl.loop(0, lines // step)
+        def _(at):
+            body(pl.ds(pl.multiple_of(at * step, step), step))
+
+    def screen_copy(to, owner):
+        return pltpu.make_async_remote_copy(
+            src_ref=screens_ref.at[0, pl.ds(to * lines, lines)],
+            dst_ref=angle.at[owner],
+            send_sem=out_sem.at[to],
+            recv_sem=in_sem.at[owner],
+            device_id={"depth": to, "trans": trans_at},
+            device_id_type=pl.DeviceIdType.MESH,
+        )
+
+    def grad_copy(to, owner):
+        return pltpu.make_async_remote_copy(
+            src_ref=grads.at[to],
+            dst_ref=out_ref.at[0, pl.ds(pl.multiple_of(owner * lines, lines), lines)],
+            send_sem=back_out_sem.at[to],
+            recv_sem=back_in_sem.at[owner],
+            device_id={"depth": to, "trans": trans_at},
+            device_id_type=pl.DeviceIdType.MESH,
+        )
+
+    def grad_start(to):
+        @pl.when(depth_at != to)
+        def _():
+            grad_copy(to, depth_at).start()
+
+        @pl.when(depth_at == to)
+        def _():
+            out_ref[0, pl.ds(to * lines, lines)] = grads[to]
+
+    barrier = pltpu.get_barrier_semaphore()
+
+    @pl.loop(0, count)
     def _(at):
-        here = pl.ds(pl.multiple_of(at * step, step), step)
-        re, im = chunk_pass(x_ref[0, here], x_ref[1, here], dft_ref, phase_ref, sign)
-        out_ref[0, here] = re
-        out_ref[1, here] = im
-
-
-def line_pass(field, tables, sign):
+        @pl.when(at != me)
+        def _():
+            pl.semaphore_signal(
+                barrier, inc=1, device_id=device(at), device_id_type=pl.DeviceIdType.MESH
+            )
+
+    pl.semaphore_wait(barrier, count - 1)
+
+    for to in range(depth_count):
+        @pl.when(depth_at != to)
+        def _():
+            screen_copy(to, depth_at).start()
+
+        @pl.when(depth_at == to)
+        def _():
+            angle[to] = screens_ref[0, pl.ds(to * lines, lines)]
+
+    def start_field(here):
+        field[0, here] = wave_ref[0, here]
+        field[1, here] = wave_ref[1, here]
+
+    chunks(start_field)
+    for to in range(depth_count):
+        @pl.when(depth_at != to)
+        def _():
+            screen_copy(to, to).wait_recv()
+            screen_copy(to, to).wait_send()
+
+    turn_start(2, angle.at[1], angle.at[3])
+
+    @pl.loop(0, depth_count)
+    def _(g):
+        @pl.when(g == 1)
+        def _():
+            turn_wait(2)
+
+            def unpack(here):
+                angle[1, here], angle[3, here] = arrived(2, here)
+
+            chunks(unpack)
+
+        def before(here):
+            c, s = cos_sin(angle[g, here])
+            r, i = field[0, here], field[1, here]
+            r, i = r * c - i * s, r * s + i * c
+            kept[g, 0, here] = r
+            kept[g, 1, here] = i
+            result[0, here], result[1, here] = chunk_pass(r, i, dft_ref, phase_ref, 1.0)
+
+        def after(here):
+            r, i = arrived(g % 2, here)
+            field[0, here], field[1, here] = chunk_pass(r, i, dft_ref, phase_ref, 1.0)
+
+        chunks(before)
+        turn_start(g % 2, result.at[0], result.at[1])
+        turn_wait(g % 2)
+        chunks(after)
+
+    def residual(here):
+        field[0, here] = field[0, here] - target_ref[0, here]
+        field[1, here] = field[1, here] - target_ref[1, here]
+
+    chunks(residual)
+
+    @pl.loop(0, depth_count)
+    def _(at):
+        g = depth_count - 1 - at
+
+        def before(here):
+            result[0, here], result[1, here] = chunk_pass(
+                field[0, here], field[1, here], dft_ref, phase_ref, -1.0
+            )
+
+        def after(here):
+            r, i = arrived(at % 2, here)
+            r, i = chunk_pass(r, i, dft_ref, phase_ref, -1.0)
+            grads[g, here] = i * kept[g, 0, here] - r * kept[g, 1, here]
+            c, s = cos_sin(angle[g, here])
+            field[0, here] = r * c + i * s
+            field[1, here] = i * c - r * s
+
+        chunks(before)
+        turn_start(at % 2, result.at[0], result.at[1])
+        turn_wait(at % 2)
+        chunks(after)
+
+        @pl.when(g == 2)
+        def _():
+            grad_start(2)
+
+        @pl.when(g == 1)
+        def _():
+            turn_start(3, grads.at[1], grads.at[3])
+
+    grad_start(0)
+    turn_wait(3)
+
+    def unpack(here):
+        grads[1, here], grads[3, here] = arrived(3, here)
+
+    chunks(unpack)
+    grad_start(1)
+    grad_start(3)
+    for to in range(depth_count):
+        @pl.when(depth_at != to)
+        def _():
+            grad_copy(to, to).wait_recv()
+            grad_copy(to, to).wait_send()
+
+
+def whole_chain(screens, wave, target, tables, depth_count):
+    two, lines, cells = wave.shape
+    count = cells // lines
+    f32 = jnp.float32
     whole = pl.BlockSpec(memory_space=pltpu.VMEM)
     return pl.pallas_call(
-        functools.partial(pass_kernel, sign),
-        out_shape=jax.ShapeDtypeStruct(field.shape, jnp.float32),
-        in_specs=[whole] * 3,
+        functools.partial(mega_kernel, depth_count),
+        out_shape=jax.ShapeDtypeStruct(screens.shape, f32),
+        in_specs=[whole] * 5,
         out_specs=whole,
-        compiler_params=pltpu.CompilerParams(vmem_limit_bytes=32 << 20),
-        name="line_pass",
-    )(field, *tables)
-
-
-def turn(field):
-    two, lines, cells = field.shape
-    count = cells // lines
-    blocks = field.reshape(two * lines, cells).T.reshape(count, lines, two * lines)
-    blocks = lax.all_to_all(blocks, AXES, split_axis=0, concat_axis=0, tiled=True)
-    blocks = blocks.reshape(count, lines, two, lines)
-    return blocks.transpose(2, 1, 0, 3).reshape(two, lines, cells)
-
-
-def rotate(field, cosine, sine):
-    return jnp.stack((field[0] * cosine - field[1] * sine, field[0] * sine + field[1] * cosine))
+        scratch_shapes=[
+            pltpu.VMEM((two, lines, cells), f32),
+            pltpu.VMEM((two, lines, cells), f32),
+            pltpu.VMEM((depth_count, two, lines, cells), f32),
+            pltpu.VMEM((depth_count, lines, cells), f32),
+            pltpu.VMEM((depth_count, lines, cells), f32),
+            pltpu.VMEM((4, count, lines, two * lines), f32),
+            pltpu.VMEM((4, count, lines, two * lines), f32),
+            pltpu.SemaphoreType.DMA((4, count)),
+            pltpu.SemaphoreType.DMA((4, count)),
+            pltpu.SemaphoreType.DMA((depth_count,)),
+            pltpu.SemaphoreType.DMA((depth_count,)),
+            pltpu.SemaphoreType.DMA((depth_count,)),
+            pltpu.SemaphoreType.DMA((depth_count,)),
+        ],
+        compiler_params=pltpu.CompilerParams(
+            collective_id=0, has_side_effects=True, vmem_limit_bytes=56 << 20
+        ),
+        name="whole_chain",
+    )(screens, wave, target, *tables)
 
 
 def illumination(angle_index, first, lines, cells):
@@ -155,29 +368,9 @@
     first = lax.axis_index("trans") * held + depth_at * lines
     tables = [jnp.asarray(t) for t in tables_of(cells)]
 
-    spread_out = screens.reshape(depth_count, lines, cells)
-    own = lax.all_to_all(spread_out, "depth", split_axis=0, concat_axis=0, tiled=True)
-    odd = turn(own[1::2])
-    phase = [odd[g // 2] if g % 2 else own[g] for g in range(depth_count)]
-    cosine, sine = [jnp.cos(p) for p in phase], [jnp.sin(p) for p in phase]
-
-    field = illumination(angle_index, first, lines, cells)
-    kept = []
-    for g in range(depth_count):
-        field = rotate(field, cosine[g], sine[g])
-        kept.append(field)
-        field = line_pass(turn(line_pass(field, tables, 1.0)), tables, 1.0)
+    wave = illumination(angle_index, first, lines, cells)
     target = lax.dynamic_slice_in_dim(measured[0], depth_at * lines, lines, 1)
-    field = field - target.astype(jnp.float32)
-    grads = [None] * depth_count
-    for g in reversed(range(depth_count)):
-        field = line_pass(turn(line_pass(field, tables, -1.0)), tables, -1.0)
-        grads[g] = field[1] * kept[g][0] - field[0] * kept[g][1]
-        field = rotate(field, cosine[g], -sine[g])
-    odd = turn(jnp.stack(grads[1::2]))
-    rows = jnp.stack([odd[g // 2] if g % 2 else grads[g] for g in range(depth_count)])
-    out = lax.all_to_all(rows, "depth", split_axis=0, concat_axis=0, tiled=True)
-    return out.reshape(1, held, cells)
+    return whole_chain(screens, wave, target.astype(jnp.float32), tables, depth_count)
 
 
 def solution(mesh):

time: 497 us -> 354 us (0.71)
  Pallas kernels: 43.5 us -> 338 us
  blocking collectives: 148 us -> 0 us
  waiting for transfers between devices: 146 us -> 0 us
  local copies, waits for them, and re-layouts: 102 us -> 4.48 us
  starting transfers between devices: 35.3 us -> 0 us
  other arithmetic: 15.3 us -> 4.78 us
    pallas_call x16 -> x1, Pallas kernels: 43.5 us -> 338 us  [whole_chain(): pl.pallas_call(functools.partial(mega_kernel, depth_count), out_shape=jax...]
    all_to_all x5 -> x0, blocking collectives: 148 us -> none  [the longest x4 120 us: turn(): lax.all_to_all(blocks, AXES, split_axis=0, concat_axis=0, tiled=True)]
    all_to_all x7 -> x0, waiting for transfers between devices: 146 us -> none  [the longest x6 124 us: turn(): lax.all_to_all(blocks, AXES, split_axis=0, concat_axis=0, tiled=True)]
    reshape x29 -> x0, local copies, waits for them, and re-layouts: 55.7 us -> none  [the longest x11 28.6 us: turn(): blocks = blocks.reshape(count, lines, two, lines)]
    all_to_all x7 -> x0, starting transfers between devices: 35.3 us -> none  [the longest x6 30.9 us: turn(): lax.all_to_all(blocks, AXES, split_axis=0, concat_axis=0, tiled=True)]
    transpose x8 -> x0, local copies, waits for them, and re-layouts: 20.6 us -> none  [turn(): return blocks.transpose(2, 1, 0, 3).reshape(two, lines, cells)]
    sub x9 -> x1, other arithmetic: 13.2 us -> 0.2 us  [illumination(): return jnp.stack((cc * rc - cs * rs, cc * rs + cs * rc))]
    sin x3 -> x0, local copies, waits for them, and re-layouts: 9.72 us -> none  [on_device(): cosine, sine = ([jnp.cos(p) for p in phase], [jnp.sin(p) for p in phase])]
  transfers between devices with their start and end apart: 7 -> 0, of which waited for: 7 -> 0; matrix products, arithmetic and copies ran while one was open for 5% -> 0% of each run, Pallas kernels for 1% -> 0%
where the time goes in v2:
time: 354 us; the launch traced here: 347 us
  Pallas kernels  338 us (95%)
  other arithmetic  4.78 us (1%)
  local copies, waits for them, and re-layouts  4.48 us (1%)
    pallas_call x1, Pallas kernels, whole_chain(): pl.pallas_call(functools.partial(mega_kernel, depth_count), out_shape=jax...  338 us

profile of v2, /device:TPU:1, one launch (start us, length us, event | category | flops | bytes accessed | tf_op | source)
XLA Modules:
  0.0 347.1 jit_solution(3898029305760053050)
XLA Ops:
  0.0 1.3 fusion.14
  1.3 0.7 fusion.12
  2.0 0.7 fusion.5
  2.7 0.2 multiply_subtract_fusion
  2.9 1.1 pad_maximum_fusion.wave_ref
  4.0 2.1 bitcast_convert_fusion.target_ref
  6.1 337.8 %whole_chain.1 = f32[1,256,2048]{2,1,0:T(8,128)} custom-call(f32[1,256,2048]{2,1,0:T(8,128)} %screens_ref.1, f32[2,64,2048]{2,1,0:T(8,128)} %pad_maximum_fusion.wave_ref, f32[2,64,2048]{2,1,0:T(8,128)} %bitcast_convert_fusion.target_ref, bf16[4,256,256]{2,1,0:T(8,128)(2,1)} %constant.34.clone.dft_ref, f32[4,16,128]{2,1,0:T(8,128)} %constant.35.clone.phase_ref), custom_call_target="tpu_custom_call" | custom-call | tf_op jit(solution)/shard_map/whole_chain/pallas_call | solution.py:323
  344.0 3.1 copy.7

commit v3 on v2

--- a/solution.py
+++ b/solution.py
@@ -111,7 +111,7 @@
     depth_count,
     screens_ref, wave_ref, target_ref, dft_ref, phase_ref,
     out_ref,
-    field, result, kept, angle, grads, send, recv,
+    result, kept, angle, grads, send, recv,
     send_sem, recv_sem, out_sem, in_sem, back_out_sem, back_in_sem,
 ):
     _, lines, cells = wave_ref.shape
@@ -120,19 +120,25 @@
     depth_at, trans_at = lax.axis_index("depth"), lax.axis_index("trans")
     me = trans_at * depth_count + depth_at
     step = min(16, lines)
+    stages = lines // step
 
     def device(at):
         return {"trans": at // depth_count, "depth": at % depth_count}
 
-    def remote(slot, to, owner):
+    def remote(slot, stage, to):
         return pltpu.make_async_remote_copy(
-            src_ref=send.at[slot, to],
-            dst_ref=recv.at[slot, owner],
-            send_sem=send_sem.at[slot, to],
-            recv_sem=recv_sem.at[slot, owner],
+            src_ref=send.at[slot, stage, to],
+            dst_ref=recv.at[slot, stage, me],
+            send_sem=send_sem.at[slot],
+            recv_sem=recv_sem.at[slot, stage],
             device_id=device(to),
             device_id_type=pl.DeviceIdType.MESH,
         )
+
+    def send_to(slot, stage, to):
+        @pl.when(to != me)
+        def _():
+            remote(slot, stage, to).start()
 
     def turn_start(slot, top, bottom):
         tiles = cells // LANES
@@ -144,33 +150,41 @@
             block = jnp.concatenate([top[:, cols], bottom[:, cols]], 0).T
             for part in range(per_tile):
                 to = tile * per_tile + part
-                send[slot, to] = block[part * lines : (part + 1) * lines]
-
-                @pl.when(to != me)
-                def _():
-                    remote(slot, to, me).start()
-
-        recv[slot, me] = send[slot, me]
-
-    def turn_wait(slot):
-        @pl.loop(0, count)
+                for stage in range(stages):
+                    begin = part * lines + stage * step
+                    send[slot, stage, to] = block[begin : begin + step]
+                send_to(slot, 0, to)
+
+        for stage in range(stages):
+            recv[slot, stage, me] = send[slot, stage, me]
+
+        @pl.loop(count, stages * count)
         def _(at):
-            @pl.when(at != me)
-            def _():
-                remote(slot, at, at).wait_recv()
-                remote(slot, at, at).wait_send()
-
-    def arrived(slot, here):
-        blocks = [recv[slot, at, here] for at in range(count)]
+            send_to(slot, at // count, lax.rem(me + at, count))
+
+    def wait_stage(slot, stage):
+        part = recv.at[slot, stage, pl.ds(0, count - 1)]
+        pltpu.make_async_copy(part, part, recv_sem.at[slot, stage]).wait()
+
+    def wait_sent(slot):
+        for stage in range(stages):
+            part = send.at[slot, stage, pl.ds(0, count - 1)]
+            pltpu.make_async_copy(part, part, send_sem.at[slot]).wait()
+
+    def arrived(slot, stage):
+        blocks = [recv[slot, stage, at] for at in range(count)]
         return (
             jnp.concatenate([b[:, :lines] for b in blocks], 1),
             jnp.concatenate([b[:, lines:] for b in blocks], 1),
         )
 
     def chunks(body):
-        @pl.loop(0, lines // step)
+        @pl.loop(0, stages)
         def _(at):
-            body(pl.ds(pl.multiple_of(at * step, step), step))
+            body(at, pl.ds(pl.multiple_of(at * step, step), step))
+
+    def line_chunk(re, im, sign):
+        return chunk_pass(re, im, dft_ref, phase_ref, sign)
 
     def screen_copy(to, owner):
         return pltpu.make_async_remote_copy(
@@ -182,24 +196,27 @@
             device_id_type=pl.DeviceIdType.MESH,
         )
 
-    def grad_copy(to, owner):
+    def grad_copy(to, owner, begin, size):
+        rows = pl.ds(pl.multiple_of(owner * lines + begin, size), size)
         return pltpu.make_async_remote_copy(
-            src_ref=grads.at[to],
-            dst_ref=out_ref.at[0, pl.ds(pl.multiple_of(owner * lines, lines), lines)],
+            src_ref=grads.at[to, pl.ds(begin, size)],
+            dst_ref=out_ref.at[0, rows],
             send_sem=back_out_sem.at[to],
             recv_sem=back_in_sem.at[owner],
             device_id={"depth": to, "trans": trans_at},
             device_id_type=pl.DeviceIdType.MESH,
         )
 
-    def grad_start(to):
+    def grad_start(to, at):
+        begin = pl.multiple_of(at * step, step)
+
         @pl.when(depth_at != to)
         def _():
-            grad_copy(to, depth_at).start()
+            grad_copy(to, depth_at, begin, step).start()
 
         @pl.when(depth_at == to)
         def _():
-            out_ref[0, pl.ds(to * lines, lines)] = grads[to]
+            out_ref[0, pl.ds(to * lines + begin, step)] = grads[to, pl.ds(begin, step)]
 
     barrier = pltpu.get_barrier_semaphore()
 
@@ -222,11 +239,6 @@
         def _():
             angle[to] = screens_ref[0, pl.ds(to * lines, lines)]
 
-    def start_field(here):
-        field[0, here] = wave_ref[0, here]
-        field[1, here] = wave_ref[1, here]
-
-    chunks(start_field)
     for to in range(depth_count):
         @pl.when(depth_at != to)
         def _():
@@ -235,89 +247,110 @@
 
     turn_start(2, angle.at[1], angle.at[3])
 
-    @pl.loop(0, depth_count)
+    def enter(g, r, i, here):
+        c, s = cos_sin(angle[g, here])
+        r, i = r * c - i * s, r * s + i * c
+        kept[g, 0, here] = r
+        kept[g, 1, here] = i
+        result[0, here], result[1, here] = line_chunk(r, i, 1.0)
+
+    def leave(g, r, i, here):
+        grads[g, here] = i * kept[g, 0, here] - r * kept[g, 1, here]
+
+    def first(at, here):
+        enter(0, wave_ref[0, here], wave_ref[1, here], here)
+
+    chunks(first)
+    turn_start(0, result.at[0], result.at[1])
+
+    def unpack_screens(at, here):
+        wait_stage(2, at)
+        angle[1, here], angle[3, here] = arrived(2, at)
+
+    chunks(unpack_screens)
+    wait_sent(2)
+
+    @pl.loop(1, depth_count)
     def _(g):
+        slot = (g - 1) % 2
+
+        def body(at, here):
+            wait_stage(slot, at)
+            r, i = line_chunk(*arrived(slot, at), 1.0)
+            enter(g, r, i, here)
+
+        chunks(body)
+        wait_sent(slot)
+        turn_start(g % 2, result.at[0], result.at[1])
+
+    last = (depth_count - 1) % 2
+
+    def residual(at, here):
+        wait_stage(last, at)
+        r, i = line_chunk(*arrived(last, at), 1.0)
+        r, i = r - target_ref[0, here], i - target_ref[1, here]
+        result[0, here], result[1, here] = line_chunk(r, i, -1.0)
+
+    chunks(residual)
+    wait_sent(last)
+    turn_start(1 - last, result.at[0], result.at[1])
+
+    @pl.loop(1, depth_count)
+    def _(turned):
+        g = depth_count - turned
+        slot = (last + turned) % 2
+
+        def body(at, here):
+            wait_stage(slot, at)
+            r, i = line_chunk(*arrived(slot, at), -1.0)
+            leave(g, r, i, here)
+            c, s = cos_sin(angle[g, here])
+            r, i = r * c + i * s, i * c - r * s
+            result[0, here], result[1, here] = line_chunk(r, i, -1.0)
+
+            @pl.when(g == 2)
+            def _():
+                grad_start(2, at)
+
+        chunks(body)
+        wait_sent(slot)
+
         @pl.when(g == 1)
         def _():
-            turn_wait(2)
-
-            def unpack(here):
-                angle[1, here], angle[3, here] = arrived(2, here)
-
-            chunks(unpack)
-
-        def before(here):
-            c, s = cos_sin(angle[g, here])
-            r, i = field[0, here], field[1, here]
-            r, i = r * c - i * s, r * s + i * c
-            kept[g, 0, here] = r
-            kept[g, 1, here] = i
-            result[0, here], result[1, here] = chunk_pass(r, i, dft_ref, phase_ref, 1.0)
-
-        def after(here):
-            r, i = arrived(g % 2, here)
-            field[0, here], field[1, here] = chunk_pass(r, i, dft_ref, phase_ref, 1.0)
-
-        chunks(before)
-        turn_start(g % 2, result.at[0], result.at[1])
-        turn_wait(g % 2)
-        chunks(after)
-
-    def residual(here):
-        field[0, here] = field[0, here] - target_ref[0, here]
-        field[1, here] = field[1, here] - target_ref[1, here]
-
-    chunks(residual)
-
-    @pl.loop(0, depth_count)
-    def _(at):
-        g = depth_count - 1 - at
-
-        def before(here):
-            result[0, here], result[1, here] = chunk_pass(
-                field[0, here], field[1, here], dft_ref, phase_ref, -1.0
-            )
-
-        def after(here):
-            r, i = arrived(at % 2, here)
-            r, i = chunk_pass(r, i, dft_ref, phase_ref, -1.0)
-            grads[g, here] = i * kept[g, 0, here] - r * kept[g, 1, here]
-            c, s = cos_sin(angle[g, here])
-            field[0, here] = r * c + i * s
-            field[1, here] = i * c - r * s
-
-        chunks(before)
-        turn_start(at % 2, result.at[0], result.at[1])
-        turn_wait(at % 2)
-        chunks(after)
-
-        @pl.when(g == 2)
-        def _():
-            grad_start(2)
-
-        @pl.when(g == 1)
-        def _():
             turn_start(3, grads.at[1], grads.at[3])
 
-    grad_start(0)
-    turn_wait(3)
-
-    def unpack(here):
-        grads[1, here], grads[3, here] = arrived(3, here)
-
-    chunks(unpack)
-    grad_start(1)
-    grad_start(3)
+        turn_start(1 - slot, result.at[0], result.at[1])
+
+    def unpack_grads(at, here):
+        wait_stage(3, at)
+        grads[1, here], grads[3, here] = arrived(3, at)
+        grad_start(1, at)
+        grad_start(3, at)
+
+    chunks(unpack_grads)
+    wait_sent(3)
+    slot = (last + depth_count) % 2
+
+    def final(at, here):
+        wait_stage(slot, at)
+        r, i = line_chunk(*arrived(slot, at), -1.0)
+        leave(0, r, i, here)
+        grad_start(0, at)
+
+    chunks(final)
+    wait_sent(slot)
     for to in range(depth_count):
         @pl.when(depth_at != to)
         def _():
-            grad_copy(to, to).wait_recv()
-            grad_copy(to, to).wait_send()
+            grad_copy(to, to, 0, lines).wait_recv()
+            grad_copy(to, to, 0, lines).wait_send()
 
 
 def whole_chain(screens, wave, target, tables, depth_count):
     two, lines, cells = wave.shape
     count = cells // lines
+    step = min(16, lines)
+    stages = lines // step
     f32 = jnp.float32
     whole = pl.BlockSpec(memory_space=pltpu.VMEM)
     return pl.pallas_call(
@@ -327,14 +360,13 @@
         out_specs=whole,
         scratch_shapes=[
             pltpu.VMEM((two, lines, cells), f32),
-            pltpu.VMEM((two, lines, cells), f32),
             pltpu.VMEM((depth_count, two, lines, cells), f32),
             pltpu.VMEM((depth_count, lines, cells), f32),
             pltpu.VMEM((depth_count, lines, cells), f32),
-            pltpu.VMEM((4, count, lines, two * lines), f32),
-            pltpu.VMEM((4, count, lines, two * lines), f32),
-            pltpu.SemaphoreType.DMA((4, count)),
-            pltpu.SemaphoreType.DMA((4, count)),
+            pltpu.VMEM((4, stages, count, step, two * lines), f32),
+            pltpu.VMEM((4, stages, count, step, two * lines), f32),
+            pltpu.SemaphoreType.DMA((4,)),
+            pltpu.SemaphoreType.DMA((4, stages)),
             pltpu.SemaphoreType.DMA((depth_count,)),
             pltpu.SemaphoreType.DMA((depth_count,)),
             pltpu.SemaphoreType.DMA((depth_count,)),

time: 354 us -> 305 us (0.86)
  Pallas kernels: 338 us -> 290 us
    pallas_call x1, Pallas kernels: 338 us -> 290 us  [whole_chain(): pl.pallas_call(functools.partial(mega_kernel, depth_count), out_shape=jax...]
where the time goes in v3:
time: 305 us; the launch traced here: 300 us
  Pallas kernels  290 us (95%)
  other arithmetic  4.78 us (2%)
  local copies, waits for them, and re-layouts  4.48 us (1%)
    pallas_call x1, Pallas kernels, whole_chain(): pl.pallas_call(functools.partial(mega_kernel, depth_count), out_shape=jax...  290 us

profile of v3, /device:TPU:1, one launch (start us, length us, event | category | flops | bytes accessed | tf_op | source)
XLA Modules:
  0.0 299.5 jit_solution(12039515310028569567)
XLA Ops:
  0.0 1.3 fusion.14
  1.3 0.7 fusion.12
  2.0 0.7 fusion.5
  2.7 0.2 multiply_subtract_fusion
  2.9 1.1 pad_maximum_fusion.wave_ref
  4.0 2.1 bitcast_convert_fusion.target_ref
  6.1 290.2 %whole_chain.1 = f32[1,256,2048]{2,1,0:T(8,128)} custom-call(f32[1,256,2048]{2,1,0:T(8,128)} %screens_ref.1, f32[2,64,2048]{2,1,0:T(8,128)} %pad_maximum_fusion.wave_ref, f32[2,64,2048]{2,1,0:T(8,128)} %bitcast_convert_fusion.target_ref, bf16[4,256,256]{2,1,0:T(8,128)(2,1)} %constant.34.clone.dft_ref, f32[4,16,128]{2,1,0:T(8,128)} %constant.35.clone.phase_ref), custom_call_target="tpu_custom_call" | custom-call | tf_op jit(solution)/shard_map/whole_chain/pallas_call | solution.py:356
  296.4 3.1 %copy.7 = f32[1,256,2048]{2,1,0:T(8,128)} copy(f32[1,256,2048]{2,1,0:T(8,128)} %whole_chain.1) | data formatting | bytes 4194304

commit v4 on v3

--- a/solution.py
+++ b/solution.py
@@ -143,7 +143,7 @@
     def turn_start(slot, top, bottom):
         tiles = cells // LANES
 
-        @pl.loop(0, tiles)
+        @pl.loop(0, tiles, unroll=2)
         def _(turn_at):
             tile = lax.rem(me * lines // LANES + turn_at, tiles)
             cols = pl.ds(pl.multiple_of(tile * LANES, LANES), LANES)
@@ -178,8 +178,8 @@
             jnp.concatenate([b[:, lines:] for b in blocks], 1),
         )
 
-    def chunks(body):
-        @pl.loop(0, stages)
+    def chunks(body, unroll=False):
+        @pl.loop(0, stages, unroll=unroll)
         def _(at):
             body(at, pl.ds(pl.multiple_of(at * step, step), step))
 
@@ -230,22 +230,23 @@
 
     pl.semaphore_wait(barrier, count - 1)
 
-    for to in range(depth_count):
-        @pl.when(depth_at != to)
-        def _():
-            screen_copy(to, depth_at).start()
-
-        @pl.when(depth_at == to)
-        def _():
-            angle[to] = screens_ref[0, pl.ds(to * lines, lines)]
-
-    for to in range(depth_count):
-        @pl.when(depth_at != to)
-        def _():
-            screen_copy(to, to).wait_recv()
-            screen_copy(to, to).wait_send()
-
-    turn_start(2, angle.at[1], angle.at[3])
+    def share_screen():
+        for to in range(depth_count):
+            @pl.when(depth_at != to)
+            def _():
+                screen_copy(to, depth_at).start()
+
+            @pl.when(depth_at == to)
+            def _():
+                angle[to] = screens_ref[0, pl.ds(to * lines, lines)]
+
+    @pl.when(depth_at == 0)
+    def _():
+        share_screen()
+
+    @pl.when(depth_at != 0)
+    def _():
+        screen_copy(0, 0).wait_recv()
 
     def enter(g, r, i, here):
         c, s = cos_sin(angle[g, here])
@@ -260,15 +261,21 @@
     def first(at, here):
         enter(0, wave_ref[0, here], wave_ref[1, here], here)
 
-    chunks(first)
+    chunks(first, True)
     turn_start(0, result.at[0], result.at[1])
 
-    def unpack_screens(at, here):
-        wait_stage(2, at)
-        angle[1, here], angle[3, here] = arrived(2, at)
-
-    chunks(unpack_screens)
-    wait_sent(2)
+    @pl.when(depth_at != 0)
+    def _():
+        share_screen()
+
+    for to in range(depth_count):
+        @pl.when(depth_at != to)
+        def _():
+            if to:
+                screen_copy(to, to).wait_recv()
+            screen_copy(to, to).wait_send()
+
+    turn_start(2, angle.at[1], angle.at[3])
 
     @pl.loop(1, depth_count)
     def _(g):
@@ -277,10 +284,21 @@
         def body(at, here):
             wait_stage(slot, at)
             r, i = line_chunk(*arrived(slot, at), 1.0)
+
+            @pl.when(g == 1)
+            def _():
+                wait_stage(2, at)
+                angle[1, here], angle[3, here] = arrived(2, at)
+
             enter(g, r, i, here)
 
         chunks(body)
         wait_sent(slot)
+
+        @pl.when(g == 1)
+        def _():
+            wait_sent(2)
+
         turn_start(g % 2, result.at[0], result.at[1])
 
     last = (depth_count - 1) % 2

time: 305 us -> 312 us (1.023)
  Pallas kernels: 290 us -> 297 us
    pallas_call x1, Pallas kernels: 290 us -> 297 us  [whole_chain(): pl.pallas_call(functools.partial(mega_kernel, depth_count), out_shape=jax...]
where the time goes in v4:
time: 312 us; the launch traced here: 307 us
  Pallas kernels  297 us (95%)
  other arithmetic  4.78 us (2%)
  local copies, waits for them, and re-layouts  4.48 us (1%)
    pallas_call x1, Pallas kernels, whole_chain(): pl.pallas_call(functools.partial(mega_kernel, depth_count), out_shape=jax...  297 us

profile of v4, /device:TPU:1, one launch (start us, length us, event | category | flops | bytes accessed | tf_op | source)
XLA Modules:
  0.0 306.8 jit_solution(8238805662030345692)
XLA Ops:
  0.0 1.3 fusion.14
  1.3 0.7 fusion.12
  2.0 0.7 fusion.5
  2.7 0.2 multiply_subtract_fusion
  2.9 1.1 pad_maximum_fusion.wave_ref
  4.0 2.1 bitcast_convert_fusion.target_ref
  6.1 297.5 %whole_chain.1 = f32[1,256,2048]{2,1,0:T(8,128)} custom-call(f32[1,256,2048]{2,1,0:T(8,128)} %screens_ref.1, f32[2,64,2048]{2,1,0:T(8,128)} %pad_maximum_fusion.wave_ref, f32[2,64,2048]{2,1,0:T(8,128)} %bitcast_convert_fusion.target_ref, bf16[4,256,256]{2,1,0:T(8,128)(2,1)} %constant.34.clone.dft_ref, f32[4,16,128]{2,1,0:T(8,128)} %constant.35.clone.phase_ref), custom_call_target="tpu_custom_call" | custom-call | tf_op jit(solution)/shard_map/whole_chain/pallas_call | solution.py:374
  303.6 3.1 %copy.7 = f32[1,256,2048]{2,1,0:T(8,128)} copy(f32[1,256,2048]{2,1,0:T(8,128)} %whole_chain.1) | data formatting | bytes 4194304

commit v5 on v3

--- a/solution.py
+++ b/solution.py
@@ -143,7 +143,7 @@
     def turn_start(slot, top, bottom):
         tiles = cells // LANES
 
-        @pl.loop(0, tiles)
+        @pl.loop(0, tiles, unroll=2)
         def _(turn_at):
             tile = lax.rem(me * lines // LANES + turn_at, tiles)
             cols = pl.ds(pl.multiple_of(tile * LANES, LANES), LANES)
@@ -178,8 +178,8 @@
             jnp.concatenate([b[:, lines:] for b in blocks], 1),
         )
 
-    def chunks(body):
-        @pl.loop(0, stages)
+    def chunks(body, unroll=False):
+        @pl.loop(0, stages, unroll=unroll)
         def _(at):
             body(at, pl.ds(pl.multiple_of(at * step, step), step))
 
@@ -260,7 +260,7 @@
     def first(at, here):
         enter(0, wave_ref[0, here], wave_ref[1, here], here)
 
-    chunks(first)
+    chunks(first, True)
     turn_start(0, result.at[0], result.at[1])
 
     def unpack_screens(at, here):

time: 305 us -> 305 us (level)
  no operation moved by 1% of the time
where the time goes in v5:
time: 305 us; the launch traced here: 300 us
  Pallas kernels  290 us (95%)
  other arithmetic  4.78 us (2%)
  local copies, waits for them, and re-layouts  4.48 us (1%)
    pallas_call x1, Pallas kernels, whole_chain(): pl.pallas_call(functools.partial(mega_kernel, depth_count), out_shape=jax...  290 us

profile of v5, /device:TPU:1, one launch (start us, length us, event | category | flops | bytes accessed | tf_op | source)
XLA Modules:
  0.0 299.5 jit_solution(3231369913209125930)
XLA Ops:
  0.0 1.3 fusion.14
  1.3 0.7 fusion.12
  2.0 0.7 fusion.5
  2.7 0.2 multiply_subtract_fusion
  2.9 1.1 pad_maximum_fusion.wave_ref
  4.0 2.1 bitcast_convert_fusion.target_ref
  6.1 290.2 %whole_chain.1 = f32[1,256,2048]{2,1,0:T(8,128)} custom-call(f32[1,256,2048]{2,1,0:T(8,128)} %screens_ref.1, f32[2,64,2048]{2,1,0:T(8,128)} %pad_maximum_fusion.wave_ref, f32[2,64,2048]{2,1,0:T(8,128)} %bitcast_convert_fusion.target_ref, bf16[4,256,256]{2,1,0:T(8,128)(2,1)} %constant.34.clone.dft_ref, f32[4,16,128]{2,1,0:T(8,128)} %constant.35.clone.phase_ref), custom_call_target="tpu_custom_call" | custom-call | tf_op jit(solution)/shard_map/whole_chain/pallas_call | solution.py:356
  296.4 3.1 %copy.7 = f32[1,256,2048]{2,1,0:T(8,128)} copy(f32[1,256,2048]{2,1,0:T(8,128)} %whole_chain.1) | data formatting | bytes 4194304
